TPU v7x, 512 devices: a whole 4x4x16 slice. The times are simulated.
512 devices in a mesh: cache: 32 (over z, core), head: 16 (over x, y).
Axes of the slice: x: 4, y: 4, z: 16, core: 2. Of those that a mesh axis runs over, the one named last changes fastest.
Arguments:
- hidden: bfloat16 [16384, 8192], P('cache', 'head'), may hold values from -6 to 6
- slot_owner: int32 [64], P('cache'), may hold values from 0 to 31, as said below
- slot_rows: int32 [64], P('cache'), may hold values from 1 to 256
- new_hidden: bfloat16 [2, 32, 8192], P(None, None, 'cache'), may hold values from -9 to 9
- w_query: bfloat16 [8192, 4096], P('cache', 'head'), may hold values from -2 to 2
- w_key: bfloat16 [8192, 4096], P('cache', 'head'), may hold values from -1 to 1
- w_value: bfloat16 [8192, 4096], P('cache', 'head'), may hold values from -0.0625 to 0.0625
- w_out: bfloat16 [4096, 8192], P('head', 'cache'), may hold values from -0.1875 to 0.1875
Outputs:
- key_cache: bfloat16 [16384, 4096], P('cache', 'head')
- value_cache: bfloat16 [16384, 4096], P('cache', 'head')
- step_out: bfloat16 [2, 32, 8192], P(None, None, ('cache', 'head'))
Inputs may be any that keep to these rules, and one draw needn't show every extreme that they name: `slot_owner`: every conversation owns at least one stored block.
All inputs are finite; a program needn't handle non-finite values.
Results may differ from a plain program's by a relative error of at most 0.035.
Values may be sent and summed in bfloat16 or wider, within the bound.
A program may use at most 64 MiB of HBM per device.

v0:
```python
import jax
import jax.numpy as jnp
from jax import lax
from jax.sharding import PartitionSpec as P

HD = 128
STEPS = 2


floor_score = -1e30


def joined_2(value, axis, combine):
    everything = jax.tree.map(
        lambda part, kind: lax.all_gather(part.astype(kind), axis),
        value,
        jax.tree.map(lambda a: jnp.bfloat16 if a.dtype == jnp.float32 else a.dtype, value),
    )

    def take(k):
        return jax.tree.map(lambda part, own: part[k].astype(own.dtype), everything, value)

    return lax.fori_loop(
        1, lax.axis_size(axis), lambda k, so_far: combine(so_far, take(k)), take(0)
    )


def combine(first_state, second_state):
    peak_one, mass_one, accum_one = first_state
    peak_two, mass_two, accum_two = second_state
    peak_both = jnp.maximum(peak_one, peak_two)
    factor_one = jnp.exp(peak_one - peak_both)
    factor_two = jnp.exp(peak_two - peak_both)
    mass_both = mass_one * factor_one + mass_two * factor_two
    accum_both = accum_one * factor_one[..., None] + accum_two * factor_two[..., None]
    return (peak_both, mass_both, accum_both)


def on_device(hidden, slot_owner, slot_rows, new_hidden, w_query, w_key, w_value, w_out):
    kv_width = w_key.shape[1]
    heads_local = kv_width // HD
    rows_local = hidden.shape[0]
    slots_local = slot_owner.shape[0]
    block_rows = rows_local // slots_local
    cache_count = lax.axis_size("cache")
    conv_total = new_hidden.shape[1]
    conv_local = conv_total // cache_count
    scale = HD ** (-0.5)
    gathered = lax.all_gather(hidden, "head", axis=1, tiled=True)
    key_part = jnp.dot(
        gathered,
        lax.all_gather(w_key, "cache", axis=0, tiled=True),
        preferred_element_type=jnp.float32,
    )
    value_part = jnp.dot(
        gathered,
        lax.all_gather(w_value, "cache", axis=0, tiled=True),
        preferred_element_type=jnp.float32,
    )
    within = jnp.arange(block_rows)[None, :] < slot_rows[:, None]
    live = within.reshape(rows_local, 1).astype(jnp.float32)
    key_cache = (key_part * live).astype(jnp.bfloat16)
    value_cache = (value_part * live).astype(jnp.bfloat16)
    slot_keys = key_cache.reshape(slots_local, block_rows, heads_local, HD)
    slot_values = value_cache.reshape(slots_local, block_rows, heads_local, HD).astype(jnp.float32)
    within_heads = within[:, :, None]
    owner_match = slot_owner[:, None] == jnp.arange(conv_total)[None, :]
    owner_select = owner_match.astype(jnp.bfloat16)
    conv_first = lax.axis_index("cache") * conv_local
    w_joined = jnp.concatenate([w_query, w_key, w_value], axis=1)
    tokens = new_hidden[0]
    fresh = []
    results = []
    for step_index in range(STEPS):

        def project(start, count, source=tokens):
            return jnp.dot(source, w_joined, preferred_element_type=jnp.float32)

        joined = lax.psum_scatter(
            project(jnp.int32(0), conv_local * lax.axis_size("cache")).astype(jnp.bfloat16),
            "cache",
            scatter_dimension=0,
            tiled=True,
        ).astype(jnp.float32)
        query = joined[:, :kv_width].astype(jnp.bfloat16)
        fresh_key = joined[:, kv_width : 2 * kv_width].astype(jnp.bfloat16)
        fresh_value = joined[:, 2 * kv_width :].astype(jnp.bfloat16)
        fresh.append((fresh_key, fresh_value))
        query_all = lax.all_gather(query, "cache", axis=0, tiled=True)
        slot_query = jnp.dot(owner_select, query_all, preferred_element_type=jnp.float32).astype(
            jnp.bfloat16
        )
        slot_query = slot_query.reshape(slots_local, heads_local, HD)
        scores = (
            jnp.einsum("sbhd,shd->sbh", slot_keys, slot_query, preferred_element_type=jnp.float32)
            * scale
        )
        scores = jnp.where(within_heads, scores, floor_score)
        slot_peak = jnp.max(scores, axis=1)
        weights = jnp.exp(scores - slot_peak[:, None, :])
        slot_mass = jnp.sum(weights, axis=1)
        slot_accum = jnp.einsum(
            "sbh,sbhd->shd", weights, slot_values, precision=lax.Precision.HIGHEST
        )
        table = (
            jnp.full((conv_total, heads_local), floor_score, jnp.float32),
            jnp.zeros((conv_total, heads_local), jnp.float32),
            jnp.zeros((conv_total, heads_local, HD), jnp.float32),
        )
        for slot_index in range(slots_local):
            merged_row = combine(
                table,
                (
                    slot_peak[slot_index][None],
                    slot_mass[slot_index][None],
                    slot_accum[slot_index][None],
                ),
            )
            chosen = owner_match[slot_index][:, None]
            table = (
                jnp.where(chosen, merged_row[0], table[0]),
                jnp.where(chosen, merged_row[1], table[1]),
                jnp.where(chosen[..., None], merged_row[2], table[2]),
            )
        merged = joined_2(table, "cache", combine)
        state = (
            lax.dynamic_slice_in_dim(merged[0], conv_first, conv_local, 0),
            lax.dynamic_slice_in_dim(merged[1], conv_first, conv_local, 0),
            lax.dynamic_slice_in_dim(merged[2], conv_first, conv_local, 0),
        )
        query_own = query.astype(jnp.float32).reshape(conv_local, heads_local, HD)
        for older_key, older_value in fresh:
            key_heads = older_key.astype(jnp.float32).reshape(conv_local, heads_local, HD)
            value_heads = older_value.astype(jnp.float32).reshape(conv_local, heads_local, HD)
            own_score = jnp.sum(query_own * key_heads, axis=-1) * scale
            state = combine(state, (own_score, jnp.ones_like(own_score), value_heads))
        attention = (
            (state[2] / state[1][..., None]).reshape(conv_local, kv_width).astype(jnp.bfloat16)
        )
        attention_all = lax.all_gather(attention, "cache", axis=0, tiled=True)
        partial_out = jnp.dot(attention_all, w_out, preferred_element_type=jnp.float32)
        share = lax.psum_scatter(
            partial_out.astype(jnp.bfloat16), "head", scatter_dimension=1, tiled=True
        )
        results.append(share)
        if step_index + 1 < STEPS:
            out_cols = lax.all_gather(share, "head", axis=1, tiled=True)
            tokens = (
                new_hidden[step_index + 1].astype(jnp.float32) + out_cols.astype(jnp.float32)
            ).astype(jnp.bfloat16)
    return (key_cache, value_cache, jnp.stack(results))


def solution(mesh):
    in_specs = (
        P("cache", "head"),
        P("cache"),
        P("cache"),
        P(None, None, "cache"),
        P("cache", "head"),
        P("cache", "head"),
        P("cache", "head"),
        P("head", "cache"),
    )
    out_specs = (P("cache", "head"), P("cache", "head"), P(None, None, ("cache", "head")))
    return jax.shard_map(
        on_device, mesh=mesh, in_specs=in_specs, out_specs=out_specs, check_vma=False
    )
```

profile of v0, /device:TPU:1, one launch (start us, length us, event | category | flops | bytes accessed | tf_op | source)
XLA Modules:
  0.0 747.6 jit_solution(13089503371816539214)
XLA Ops:
  10.9 1.3 dynamic-slice
  12.1 0.9 constant_dynamic-update-slice_fusion.2
  13.0 0.9 constant_dynamic-update-slice_fusion.1
  14.0 0.9 constant_dynamic-update-slice_fusion
  14.9 0.9 fusion.12
  15.8 99.3 %all-reduce = bf16[32,768]{1,0:T(8,128)(2,1)S(1)} all-reduce(bf16[32,768]{1,0:T(8,128)(2,1)S(1)} %fusion.12), channel_id=2, replica_groups=mesh['cache'=32,'head'=16] {'cache'}, use_global_device_ids=true, to_apply=%region_0.0.clone | all-reduce | flops 24576 | bytes 98304
  115.1 0.7 fusion.86
  115.8 30.0 %all-gather = bf16[32,1,256]{2,1,0:T(2,128)(2,1)S(1)} all-gather(bf16[1,1,256]{2,1,0:T(2,128)(2,1)S(1)} %get-tuple-element.438), channel_id=1, replica_groups=mesh['cache'=32,'head'=16] {'cache'}, dimensions={0}, use_global_device_ids=true | all-gather | bytes 16896 | tf_op jit(solution)/shard_map/all_gather | solution.py:89
  145.8 0.8 convolution_convert_fusion.5
  146.7 1.3 dynamic-slice.2
  148.0 0.7 convert_multiply_fusion.5
  150.3 31.9 %all-gather.8.cloned.1.call-done = bf16[512,8192]{1,0:T(8,128)(2,1)} async-done(((bf16[512,512]{1,0:T(8,128)(2,1)}), bf16[512,8192]{1,0:T(8,128)(2,1)}) %all-gather.8.cloned.1.call-update) | async-done | bytes 8388624 | tf_op jit(solution)/shard_map/all_gather | solution.py:49
  182.2 6.9 fusion.10
  189.8 32.2 %all_gather.52 = bf16[32,32,2]{1,2,0:T(2,128)(2,1)S(1)} all-gather(bf16[1,32,2]{1,2,0:T(2,128)(2,1)S(1)} %fusion.46), channel_id=1, replica_groups=mesh['cache'=32,'head'=16] {'cache'}, dimensions={0}, use_global_device_ids=true | all-gather | bytes 4224 | tf_op jit(solution)/shard_map/all_gather | solution.py:15
  222.0 27.9 %all_gather.53 = bf16[32,32,2]{1,2,0:T(2,128)(2,1)S(1)} all-gather(bf16[1,32,2]{1,2,0:T(2,128)(2,1)S(1)} %fusion.51), channel_id=1, replica_groups=mesh['cache'=32,'head'=16] {'cache'}, dimensions={0}, use_global_device_ids=true | all-gather | bytes 4224 | tf_op jit(solution)/shard_map/all_gather | solution.py:15
  250.0 9.2 %all-gather.12.cloned.1.call-done = bf16[8192,256]{1,0:T(8,128)(2,1)} async-done(((bf16[256,256]{1,0:T(8,128)(2,1)}), bf16[8192,256]{1,0:T(8,128)(2,1)}) %all-gather.12.cloned.1.call-update) | async-done | bytes 4194320 | tf_op jit(solution)/shard_map/all_gather | solution.py:57
  259.2 6.9 fusion.11
  266.5 30.6 %all_gather.54 = bf16[32,32,2,128]{3,1,2,0:T(8,128)(2,1)S(1)} all-gather(bf16[1,32,2,128]{3,1,2,0:T(8,128)(2,1)S(1)} %select_convert_fusion.1), channel_id=1, replica_groups=mesh['cache'=32,'head'=16] {'cache'}, dimensions={0}, use_global_device_ids=true | all-gather | bytes 540672 | tf_op jit(solution)/shard_map/all_gather | solution.py:15
  297.2 14.7 %while.38 = (s32[]{:T(128)}, f32[32,2]{0,1:T(2,128)S(1)}, f32[32,2]{0,1:T(2,128)S(1)}, f32[32,2,128]{2,1,0:T(2,128)S(1)}, bf16[32,32,2]{1,2,0:T(2,128)(2,1)S(1)}...) while((s32[]{:T(128)}, f32[32,2]{0,1:T(2,128)S(1)}, ...), condition=%wide.region_4.5_spmd, body=%wide.region_3.4_spmd.sunk | while | flops 33285 | bytes 118167 | solution.py:23
  312.1 27.1 %all-gather.1 = bf16[32,1,256]{2,1,0:T(2,128)(2,1)S(1)} all-gather(bf16[1,1,256]{2,1,0:T(2,128)(2,1)S(1)} %reshape.1294), channel_id=1, replica_groups=mesh['cache'=32,'head'=16] {'cache'}, dimensions={0}, use_global_device_ids=true | all-gather | bytes 16896 | tf_op jit(solution)/shard_map/all_gather | solution.py:140
  339.5 60.6 %all-reduce.1 = bf16[32,256]{0,1:T(8,128)(2,1)S(1)} all-reduce(bf16[32,256]{0,1:T(8,128)(2,1)S(1)} %convolution_convert_fusion.1), channel_id=3, replica_groups=mesh['cache'=32,'head'=16] {'head'}, use_global_device_ids=true, to_apply=%region_6.7.clone | all-reduce | flops 8192 | bytes 32768
  400.1 15.3 %all_gather.56 = bf16[32,256]{0,1:T(8,128)(2,1)S(1)} all-gather(bf16[32,16]{0,1:T(8,128)(2,1)S(1)} %constant_dynamic-slice_fusion.14), channel_id=1, replica_groups=mesh['cache'=32,'head'=16] {'head'}, dimensions={1}, use_global_device_ids=true | all-gather | bytes 17408 | tf_op jit(solution)/shard_map/all_gather | solution.py:147
  415.6 105.6 %all-reduce.2 = bf16[32,768]{1,0:T(8,128)(2,1)S(1)} all-reduce(bf16[32,768]{1,0:T(8,128)(2,1)S(1)} %convolution_convert_fusion.3), channel_id=4, replica_groups=mesh['cache'=32,'head'=16] {'cache'}, use_global_device_ids=true, to_apply=%region_7.8.clone | all-reduce | flops 24576 | bytes 98304
  521.3 0.7 fusion.87
  522.0 30.2 %all-gather.2 = bf16[32,1,256]{2,1,0:T(2,128)(2,1)S(1)} all-gather(bf16[1,1,256]{2,1,0:T(2,128)(2,1)S(1)} %get-tuple-element.436), channel_id=1, replica_groups=mesh['cache'=32,'head'=16] {'cache'}, dimensions={0}, use_global_device_ids=true | all-gather | bytes 16896 | tf_op jit(solution)/shard_map/all_gather | solution.py:89
  552.9 0.7 fusion.65
  553.7 28.5 %all_gather.58 = bf16[32,32,2]{1,2,0:T(2,128)(2,1)S(1)} all-gather(bf16[1,32,2]{1,2,0:T(2,128)(2,1)S(1)} %fusion.52), channel_id=1, replica_groups=mesh['cache'=32,'head'=16] {'cache'}, dimensions={0}, use_global_device_ids=true | all-gather | bytes 4224 | tf_op jit(solution)/shard_map/all_gather | solution.py:15
  582.3 26.8 %all_gather.59 = bf16[32,32,2]{1,2,0:T(2,128)(2,1)S(1)} all-gather(bf16[1,32,2]{1,2,0:T(2,128)(2,1)S(1)} %fusion.57), channel_id=1, replica_groups=mesh['cache'=32,'head'=16] {'cache'}, dimensions={0}, use_global_device_ids=true | all-gather | bytes 4224 | tf_op jit(solution)/shard_map/all_gather | solution.py:15
  609.5 29.9 %all_gather.60 = bf16[32,32,2,128]{3,1,2,0:T(8,128)(2,1)S(1)} all-gather(bf16[1,32,2,128]{3,1,2,0:T(8,128)(2,1)S(1)} %select_convert_fusion), channel_id=1, replica_groups=mesh['cache'=32,'head'=16] {'cache'}, dimensions={0}, use_global_device_ids=true | all-gather | bytes 540672 | tf_op jit(solution)/shard_map/all_gather | solution.py:15
  639.4 14.6 %while.39 = (s32[]{:T(128)}, f32[32,2]{0,1:T(2,128)S(1)}, f32[32,2]{0,1:T(2,128)S(1)}, f32[32,2,128]{2,1,0:T(2,128)S(1)}, bf16[32,32,2]{1,2,0:T(2,128)(2,1)S(1)}...) while((s32[]{:T(128)}, f32[32,2]{0,1:T(2,128)S(1)}, ...), condition=%wide.region_11.12_spmd, body=%wide.region_10.11_spmd.sunk | while | flops 33285 | bytes 118167 | solution.py:23
  654.6 27.1 %all-gather.3 = bf16[32,1,256]{2,1,0:T(2,128)(2,1)S(1)} all-gather(bf16[1,1,256]{2,1,0:T(2,128)(2,1)S(1)} %reshape.1298), channel_id=1, replica_groups=mesh['cache'=32,'head'=16] {'cache'}, dimensions={0}, use_global_device_ids=true | all-gather | bytes 16896 | tf_op jit(solution)/shard_map/all_gather | solution.py:140
  682.0 58.5 %all-reduce.3 = bf16[32,256]{0,1:T(8,128)(2,1)S(1)} all-reduce(bf16[32,256]{0,1:T(8,128)(2,1)S(1)} %convolution_convert_fusion), channel_id=5, replica_groups=mesh['cache'=32,'head'=16] {'head'}, use_global_device_ids=true, to_apply=%region_14.15.clone | all-reduce | flops 8192 | bytes 32768
  (389 shorter events, 36.7 us)
Async XLA Ops:
  7.2 332.1 %copy-start = (bf16[256,256]{1,0:T(8,128)(2,1)S(1)}, bf16[256,256]{1,0:T(8,128)(2,1)}, u32[]{:S(2)}) copy-start(bf16[256,256]{1,0:T(8,128)(2,1)} %param.19) | copy-start | bytes 393220
  7.2 143.1 %all-gather.10.cloned.1.call-start = ((), (), s32[]{:S(2)}) async-start(), calls=%async_computation.1 | async-start | bytes 4325376 | tf_op jit(solution)/shard_map/all_gather | solution.py:52
  7.9 174.2 %all-gather.8.cloned.1.call-start = ((), (), s32[]{:S(2)}) async-start(), calls=%async_computation | async-start | bytes 8912896 | tf_op jit(solution)/shard_map/all_gather | solution.py:49
  8.7 250.5 %all-gather.12.cloned.1.call-start = ((), (), s32[]{:S(2)}) async-start(), calls=%async_computation.2 | async-start | bytes 4325376 | tf_op jit(solution)/shard_map/all_gather | solution.py:57
  189.1 77.0 %copy-start.1 = (bf16[512,256]{1,0:T(8,128)(2,1)}, bf16[512,256]{1,0:T(8,128)(2,1)S(1)}, u32[]{:S(2)}) copy-start(bf16[512,256]{1,0:T(8,128)(2,1)S(1)} %fusion.10) | copy-start | bytes 786436
  250.0 302.1 %copy-start.3 = (s32[2]{0:T(128)S(1)}, s32[2]{0:T(128)}, u32[]{:S(2)}) copy-start(s32[2]{0:T(128)} %param.13) | copy-start | bytes 28
  266.1 475.0 %copy-start.2 = (bf16[512,256]{1,0:T(8,128)(2,1)}, bf16[512,256]{1,0:T(8,128)(2,1)S(1)}, u32[]{:S(2)}) copy-start(bf16[512,256]{1,0:T(8,128)(2,1)S(1)} %fusion.11) | copy-start | bytes 786436
Sparse Core Ops, SparseCore 0:
  10.1 79.7 all-gather.9
  93.0 89.1 all-gather.7
  184.3 74.8 all-gather.11
where the time goes:
time: 761 us; the launch traced here: 748 us
  blocking collectives  630 us (83%)
  waiting for transfers between devices  43.1 us (6%)
  other arithmetic  22.9 us (3%)
  local copies, waits for them, and re-layouts  18.3 us (2%)
  matrix products  17.1 us (2%)
  between operations  14.6 us (2%)
    unnamed x4, blocking collectives  324 us
    all_gather x6, blocking collectives, joined_2(): lax.all_gather(part.astype(kind), axis)  176 us
    all_gather x2, blocking collectives, on_device(): query_all = lax.all_gather(query, 'cache', axis=0, tiled=True)  60.2 us
    all_gather x2, blocking collectives, on_device(): attention_all = lax.all_gather(attention, 'cache', axis=0, tiled=True)  54.2 us
    all_gather x1, waiting for transfers between devices, on_device(): gathered = lax.all_gather(hidden, 'head', axis=1, tiled=True)  31.9 us
    all_gather x1, blocking collectives, on_device(): out_cols = lax.all_gather(share, 'head', axis=1, tiled=True)  15.3 us
  transfers between devices with their start and end apart: 3, of which 2 were waited for; matrix products, arithmetic and copies ran while one was open for 3% of the time, Pallas kernels for 0%

commit v1 on v0

v1 whole, which is shorter than its diff:
```python
import jax
import jax.numpy as jnp
from jax import lax
from jax.experimental import pallas as pl
from jax.experimental.pallas import tpu as pltpu
from jax.sharding import PartitionSpec as P

HD = 128
STEPS = 2
MESH = pl.DeviceIdType.MESH
NX, NY, NZ = 4, 4, 16
BLOCK = 256
QUARTER = 128


def place():
    c = lax.axis_index("cache")
    h = lax.axis_index("head")
    return c // 2, lax.rem(c, 2), h // NY, lax.rem(h, NY)


def at(z, k, x, y):
    return {"cache": z * 2 + k, "head": x * NY + y}


def hop(value, by, size):
    return lax.rem(value + (by + size), size)
Z_FAR_FIRST = (8, 7, -7, 6, -6, 5, -5, 4, -4, 3, -3, 2, -2, 1, -1)
PLANE_FAR_FIRST = tuple(
    sorted(
        ((dx, dy) for dx in (2, 1, -1, 0) for dy in (2, 1, -1, 0) if dx or dy),
        key=lambda d: -abs(d[0]) - abs(d[1]),
    )
)
K_NEW, K_WQ, K_WO, K_TAG_PAIR, K_TAG, K_OPAIR, K_OUT, K_LAST = range(8)
K_Q, K_KV, K_QPAIR, K_STATE, K_STATEPAIR = 8, 10, 12, 14, 16
KINDS = 18


def layer_kernel(
    owner_ref, rows_ref, hidden_ref, new_ref, wq_ref, wk_ref, wv_ref, wo_ref,
    key_ref, value_ref, out_ref,
    hbuf, wbuf, acc, kout, vout, fresh_in, wq2, wo2,
    qsend, qrecv, qpair, qall, kvsend, kvrecv, kvown, states, osend, orecv, opair, fsend, frecv,
    tags,
    hsend, hsem, wsend, wsem, sibsend, lsem, osem, msem, mrecv,
):
    z, k, x, y = place()
    me = x * NY + y
    mine = z * 2 + k
    xn = {s: at(z, k, hop(x, s, NX), y) for s in (1, -1)}
    yn = {s: at(z, k, x, hop(y, s, NY)) for s in (1, -1)}
    zn = {s: at(hop(z, s, NZ), k, x, y) for s in (1, -1)}
    sib = at(z, 1 - k, x, y)
    barrier = pltpu.get_barrier_semaphore()
    partners = [at(z, 1 - k, x, y)]
    partners += [at(hop(z, dz, NZ), k, x, y) for dz in Z_FAR_FIRST]
    partners += [at(z, k, hop(x, dx, NX), hop(y, dy, NY)) for dx, dy in PLANE_FAR_FIRST]
    for other in partners:
        pl.semaphore_signal(barrier, inc=1, device_id=other, device_id_type=MESH)
    local = [
        pltpu.make_async_copy(hidden_ref, hbuf.at[me], lsem.at[0]),
        pltpu.make_async_copy(wk_ref, wbuf.at[mine, 0], lsem.at[1]),
        pltpu.make_async_copy(wv_ref, wbuf.at[mine, 1], lsem.at[2]),
        pltpu.make_async_copy(new_ref, fresh_in.at[k], lsem.at[3]),
        pltpu.make_async_copy(wq_ref, wq2.at[k], lsem.at[4]),
        pltpu.make_async_copy(wo_ref, wo2.at[k], lsem.at[5]),
    ]
    for copy in local:
        copy.start()
    pl.semaphore_wait(barrier, len(partners))

    def source(dx, dy):
        return hop(x, dx, NX) * NY + hop(y, dy, NY)

    def push(dx, dy, piece, to, own=False):
        index = source(dx, dy)
        rows = pl.ds(piece * QUARTER, QUARTER)
        src = hidden_ref.at[rows] if own else hbuf.at[index, rows]
        pltpu.make_async_remote_copy(
            src_ref=src, dst_ref=hbuf.at[index, rows],
            send_sem=hsend, recv_sem=hsem.at[index, piece],
            device_id=to, device_id_type=MESH,
        ).start()

    def landed(dx, dy, pieces):
        index = source(dx, dy)
        for piece in pieces:
            part = hbuf.at[index, pl.ds(piece * QUARTER, QUARTER)]
            pltpu.make_async_copy(part, part, hsem.at[index, piece]).wait()

    def spread(half, a, b, axis, own=False):
        dx, dy = (a, b) if half == 0 else (b, a)
        nb = xn if axis == half else yn
        for sign in (1, -1):
            for piece in (2 * half, 2 * half + 1):
                push(dx, dy, piece, nb[sign], own)

    def relay(half, axis, other):
        nb = xn if axis == half else yn
        for sign, piece in ((1, 2 * half), (-1, 2 * half + 1)):
            step = (-sign, other) if axis == 0 else (other, -sign)
            dx, dy = step if half == 0 else step[::-1]
            push(dx, dy, piece, nb[sign])

    def got(half, a, b):
        dx, dy = (a, b) if half == 0 else (b, a)
        landed(dx, dy, (2 * half, 2 * half + 1))

    def hidden_round(r):
        for half in (0, 1):
            if r == 0:
                spread(half, 0, 0, 0, own=True)
        for half in (0, 1):
            if r == 0:
                spread(half, 0, 0, 1, own=True)
            if r == 1:
                got(half, 1, 0)
                got(half, -1, 0)
                relay(half, 0, 0)
                spread(half, -1, 0, 1)
                spread(half, 1, 0, 1)
            if r == 2:
                got(half, 0, 1)
                got(half, 0, -1)
                relay(half, 1, 0)
            if r == 3:
                got(half, 2, 0)
                spread(half, 2, 0, 1)
                got(half, 0, 2)
            if r == 4:
                got(half, -1, 1)
                got(half, -1, -1)
                relay(half, 1, -1)
            if r == 5:
                got(half, 1, 1)
                got(half, 1, -1)
                relay(half, 1, 1)
            if r == 6:
                got(half, 2, 1)
                got(half, 2, -1)
                relay(half, 1, 2)
            if r == 7:
                got(half, -1, 2)
                got(half, 1, 2)
            if r == 8:
                got(half, 2, 2)

    def ready(dx, dy):
        ax, ay = jnp.minimum(dx, NX - dx), jnp.minimum(dy, NY - dy)
        near = ax + ay
        both = jnp.where((dx == 3) & (dy == 3), 4, 5)
        far = jnp.where((ax == 2) & (ay == 2), 8, 7)
        out = jnp.where(near == 1, 2, jnp.where((ax == 0) | (ay == 0), 3, jnp.where(near == 2, both, far)))
        return jnp.where(near == 0, 0, out)

    def block(dz, core):
        return hop(z, dz, NZ) * 2 + core

    def ring(dz, chunk, to):
        part = wbuf.at[block(dz, k), chunk]
        src = (wk_ref if chunk == 0 else wv_ref) if dz == 0 else part
        pltpu.make_async_remote_copy(
            src_ref=src, dst_ref=part, send_sem=wsend, recv_sem=wsem.at[block(dz, k), chunk],
            device_id=to, device_id_type=MESH,
        ).start()

    def share(dz, chunk):
        part = wbuf.at[block(dz, k), chunk]
        src = (wk_ref if chunk == 0 else wv_ref) if dz == 0 else part
        pltpu.make_async_remote_copy(
            src_ref=src, dst_ref=part, send_sem=sibsend, recv_sem=wsem.at[block(dz, k), chunk],
            device_id=sib, device_id_type=MESH,
        ).start()

    def have(dz, core, chunk):
        part = wbuf.at[block(dz, core), chunk]
        pltpu.make_async_copy(part, part, wsem.at[block(dz, core), chunk]).wait()

    def weight_round(r):
        if r == 0:
            for chunk in (0, 1):
                for sign in (1, -1):
                    ring(0, chunk, zn[sign])
            for chunk in (0, 1):
                share(0, chunk)
        elif r < NZ // 2:
            for chunk in (0, 1):
                for sign in (1, -1):
                    have(-sign * r, k, chunk)
                    if r < NZ // 2 - 1 or (sign == 1) == (chunk == 0):
                        ring(-sign * r, chunk, zn[sign])
                    share(-sign * r, chunk)
        else:
            for chunk in (0, 1):
                have(r, k, chunk)
                share(r, chunk)

    def weight_settle(r):
        for dz in ((r, -r) if 0 < r < NZ // 2 else (r,)):
            for chunk in (0, 1):
                have(dz, 1 - k, chunk)

    def products(r, first):
        def one(h, carry):
            due = ready(hop(h // NY, NX - x, NX), hop(lax.rem(h, NY), NY - y, NY))
            away = hop(h, NZ - z, NZ)
            due = jnp.maximum(due, jnp.minimum(away, NZ - away))
            now = (due <= r) if first else (due == r)

            @pl.when(now)
            def _():
                for chunk in (0, 1):
                    part = jnp.dot(
                        hbuf[h, :, :BLOCK], wbuf[2 * h, chunk], preferred_element_type=jnp.float32
                    ) + jnp.dot(
                        hbuf[h, :, BLOCK:], wbuf[2 * h + 1, chunk], preferred_element_type=jnp.float32
                    )
                    acc[chunk] += part

            return carry

        lax.fori_loop(0, NX * NY, one, 0)

    def remote(src, dst, kind, to):
        pltpu.make_async_remote_copy(
            src_ref=src, dst_ref=dst, send_sem=msem.at[kind], recv_sem=mrecv.at[kind],
            device_id=to, device_id_type=MESH,
        ).start()

    def arrived(part, kind):
        pltpu.make_async_copy(part, part, mrecv.at[kind]).wait()

    def departed(part, kind):
        pltpu.make_async_copy(part, part, msem.at[kind]).wait()

    def along_z(src, dst, kind):
        for dz in Z_FAR_FIRST:
            remote(src, dst, kind, at(hop(z, dz, NZ), k, x, y))

    lane = lax.broadcasted_iota(jnp.int32, (1, 128), 1)
    my_row = (lax.broadcasted_iota(jnp.int32, (2, 128), 0) == k).astype(jnp.float32)

    def tag_row(values):
        row = jnp.zeros((1, 128), jnp.float32)
        for r, value in enumerate(values):
            row = jnp.where(lane == z * 8 + r, value, row)
        return row * my_row

    def pair_start():
        remote(new_ref, fresh_in.at[k], K_NEW, sib)
        remote(wq_ref, wq2.at[k], K_WQ, sib)
        remote(wo_ref, wo2.at[k], K_WO, sib)
        owners = [owner_ref[0].astype(jnp.float32), owner_ref[1].astype(jnp.float32)]
        tags[0, 6:8, :] = tag_row([owners[0], owners[0], owners[1], owners[1]])
        tags[0, 0:6, :] = jnp.zeros((6, 128), jnp.float32)
        remote(tags.at[0], tags.at[1], K_TAG_PAIR, sib)

    def pair_finish():
        arrived(fresh_in.at[k], K_NEW)
        arrived(wq2.at[k], K_WQ)
        arrived(wo2.at[k], K_WO)

    def owners_start():
        arrived(tags.at[1], K_TAG_PAIR)
        both = tags[0] + tags[1]
        tags[2] = both
        tags[3 + z] = both
        along_z(tags.at[2], tags.at[3 + z], K_TAG)

    def owners():
        total = jnp.sum(tags[3:], axis=0)
        row = jnp.concatenate([total[6:7], total[7:8]], axis=1)
        spot = lax.broadcasted_iota(jnp.int32, (1, 256), 1)
        kind = lax.rem(spot, 8)
        own = (spot // 8).astype(jnp.float32)
        return jnp.where(kind < 4, row, jnp.where(kind < 6, own, -1.0))

    def project(t, tokens):
        q = jnp.zeros((16, 256), jnp.float32)
        kv = [jnp.zeros((16, 256), jnp.float32)] * 2
        for core in (0, 1):
            q += jnp.dot(tokens[core], wq2[core], preferred_element_type=jnp.float32)
        q16 = q.astype(jnp.bfloat16)
        qsend[t] = q16
        qrecv[t, z] = q16
        along_z(qsend.at[t], qrecv.at[t, z], K_Q + t)
        for chunk in (0, 1):
            for core in (0, 1):
                kv[chunk] += jnp.dot(
                    tokens[core], wbuf[2 * z + core, chunk], preferred_element_type=jnp.float32
                )
        for chunk in (0, 1):
            for j in (0, 1):
                kvsend[t, :, 2 * chunk + j, :] = kv[chunk][:, j * HD : (j + 1) * HD]
        kvrecv[t, z] = kvsend[t, z]
        for dz in Z_FAR_FIRST:
            to = hop(z, dz, NZ)
            remote(kvsend.at[t, to], kvrecv.at[t, z], K_KV + t, at(to, k, x, y))

    def query_half(t):
        arrived(qrecv.at[t, pl.ds(0, 15)], K_Q + t)
        half = jnp.sum(qrecv[t].astype(jnp.float32), axis=0).astype(jnp.bfloat16)
        qpair[t, k] = half
        remote(qpair.at[t, k], qpair.at[t, k], K_QPAIR + t, sib)
        return half.astype(jnp.float32)

    def query_rest(t):
        arrived(qpair.at[t, 1 - k], K_QPAIR + t)
        qall[0:16, :] = qpair[t, 0].astype(jnp.float32)
        qall[16:32, :] = qpair[t, 1].astype(jnp.float32)

    def new_pair(t):
        arrived(kvrecv.at[t, pl.ds(0, 15)], K_KV + t)
        total = jnp.sum(kvrecv[t], axis=0)
        kvown[t] = total.astype(jnp.bfloat16).astype(jnp.float32)

    scale = HD ** (-0.5)
    sub2 = lax.broadcasted_iota(jnp.int32, (2, 128), 0)

    def new_state(t):
        q = qall[pl.ds(k * 16 + z, 1), :]
        q2 = jnp.where(sub2 == 0, q[:, :HD], q[:, HD:])
        scores = [
            jnp.sum(q2 * kvown[s, 0:2, :], axis=1, keepdims=True) * scale for s in range(t + 1)
        ]
        peak = scores[0]
        for s in scores[1:]:
            peak = jnp.maximum(peak, s)
        mass = jnp.zeros((2, 1), jnp.float32)
        mixed = jnp.zeros((2, HD), jnp.float32)
        for s, score in enumerate(scores):
            w = jnp.exp(score - peak)
            mass += w
            mixed += w * kvown[s, 2:4, :]
        return mixed / mass, peak + jnp.log(mass)

    def slot_state(i):
        rows = pl.ds(i * BLOCK, BLOCK)
        q = qall[pl.ds(owner_ref[i], 1), :]
        spot = lax.broadcasted_iota(jnp.int32, (8, 256), 1)
        line = lax.broadcasted_iota(jnp.int32, (8, 256), 0)
        q2 = jnp.where(spot // HD == line, q, 0.0).astype(jnp.bfloat16)
        scores = lax.dot_general(
            q2, kout[rows, :], (((1,), (1,)), ((), ())), preferred_element_type=jnp.float32
        )
        scores = jnp.where(spot < rows_ref[i], scores * scale, -1e30)
        peak = jnp.max(scores, axis=1, keepdims=True)
        w = jnp.exp(scores - peak)
        mass = jnp.sum(w, axis=1, keepdims=True)
        mixed = jnp.dot(w.astype(jnp.bfloat16), vout[rows, :], preferred_element_type=jnp.float32)
        mixed = mixed / mass
        lse = peak + jnp.log(mass)
        return jnp.where(sub2 == 0, mixed[0:2, :HD], mixed[0:2, HD:]), lse[0:2]

    def exchange_states(t):
        tag = []
        for i in range(3):
            mixed, lse = slot_state(i) if i < 2 else new_state(t)
            states[t, k, z, 2 * i : 2 * i + 2, :] = mixed
            tag += [lse[0:1], lse[1:2]]
        states[t, k, z, 6:8, :] = tag_row(tag)
        along_z(states.at[t, k, z], states.at[t, k, z], K_STATE + t)
        arrived(states.at[t, k, pl.ds(0, 15)], K_STATE + t)
        remote(states.at[t, k], states.at[t, k], K_STATEPAIR + t, sib)
        arrived(states.at[t, 1 - k], K_STATEPAIR + t)

    def attention(t, owner, first, count):
        held = states[t].reshape(256, 128)
        total = jnp.sum(states[t].reshape(32, 8, 128), axis=0)
        lse = jnp.concatenate([total[6:7], total[7:8]], axis=1)
        spot = lax.broadcasted_iota(jnp.int32, (count, 256), 1)
        conv = (lax.broadcasted_iota(jnp.int32, (count, 256), 0) + first).astype(jnp.float32)
        mine_ = owner == conv
        held = held.astype(jnp.bfloat16)
        parts = []
        for j in (0, 1):
            valid = mine_ & (lax.rem(spot, 2) == j)
            kept = jnp.where(valid, lse, -1e30)
            peak = jnp.max(kept, axis=1, keepdims=True)
            w = jnp.where(valid, jnp.exp(kept - peak), 0.0)
            w = w / jnp.sum(w, axis=1, keepdims=True)
            parts.append(
                jnp.dot(w.astype(jnp.bfloat16), held, preferred_element_type=jnp.float32)
            )
        return jnp.concatenate(parts, axis=1).astype(jnp.bfloat16)

    def plane(pick, dst, kind):
        for dx, dy in PLANE_FAR_FIRST:
            to = source(dx, dy)
            remote(pick(to), dst, kind, at(z, k, hop(x, dx, NX), hop(y, dy, NY)))

    def next_tokens(owner):
        half = attention(0, owner, 16 * k, 16)
        for core in (0, 1):
            part = jnp.dot(half, wo2[core], preferred_element_type=jnp.float32).astype(jnp.bfloat16)
            osend[core] = part
            orecv[me, core] = part
        plane(lambda to: osend, orecv.at[me], K_OUT)
        arrived(orecv.at[pl.ds(0, 15)], K_OUT)
        tokens = []
        for core in (0, 1):
            out = jnp.sum(orecv[:, core].astype(jnp.float32), axis=0).astype(jnp.bfloat16)
            opair[k, core] = out
            tokens.append(
                (fresh_in[core, 1, k].astype(jnp.float32) + out.astype(jnp.float32)).astype(
                    jnp.bfloat16
                )
            )
        return tokens

    def own_columns(value, width, start):
        pick = lax.broadcasted_iota(jnp.int32, (width, 16), 0) == (
            lax.broadcasted_iota(jnp.int32, (width, 16), 1) + start
        )
        return jnp.dot(
            value, pick.astype(jnp.bfloat16), preferred_element_type=jnp.float32
        ).astype(jnp.bfloat16)

    def last_output(owner):
        both = attention(1, owner, 0, 32)
        part = jnp.dot(both, wo2[k], preferred_element_type=jnp.float32).astype(jnp.bfloat16)
        for side in (0, 1):
            fsend[side] = part[:, side * 128 : (side + 1) * 128]
        frecv[me] = fsend[me // 8]
        plane(lambda to: fsend.at[to // 8], frecv.at[me], K_LAST)
        for half in (0, 1):
            out_ref[0, 16 * half : 16 * half + 16, :] = own_columns(opair[half, k], 256, me * 16)
        arrived(frecv.at[pl.ds(0, 15)], K_LAST)
        out = jnp.sum(frecv[...].astype(jnp.float32), axis=0).astype(jnp.bfloat16)
        out_ref[1] = own_columns(out, 128, lax.rem(me, 8) * 16)

    for chunk in (0, 1):
        acc[chunk] = jnp.zeros(acc.shape[1:], jnp.float32)
    for r in range(9):
        weight_round(r)
        hidden_round(r)
        if r == 0:
            pair_start()
            for copy in local:
                copy.wait()
            pair_finish()
        weight_settle(r)
        if r == 0:
            project(0, [fresh_in[0, 0, k], fresh_in[1, 0, k]])
            owners_start()
        if r == 4:
            query_half(0)
        if r == 5:
            query_rest(0)
            new_pair(0)
        if r == 6:
            arrived(tags.at[pl.ds(3, 15)], K_TAG)
        if r >= 2:
            products(r, r == 2)
    for slot in (0, 1):
        rows = pl.ds(slot * BLOCK, BLOCK)
        keep = lax.broadcasted_iota(jnp.int32, (BLOCK, BLOCK), 0) < rows_ref[slot]
        for chunk, out in ((0, kout), (1, vout)):
            out[rows, :] = jnp.where(keep, acc[chunk, rows, :], 0.0).astype(jnp.bfloat16)
    outs = [
        pltpu.make_async_copy(kout, key_ref, osem.at[0]),
        pltpu.make_async_copy(vout, value_ref, osem.at[1]),
    ]
    for copy in outs:
        copy.start()
    owner = owners()
    exchange_states(0)
    tokens = next_tokens(owner)
    project(1, tokens)
    remote(opair.at[k, 1 - k], opair.at[k, 1 - k], K_OPAIR, sib)
    query_half(1)
    new_pair(1)
    query_rest(1)
    exchange_states(1)
    arrived(opair.at[1 - k, k], K_OPAIR)
    last_output(owner)

    pltpu.make_async_copy(hbuf.at[pl.ds(0, 15)], hbuf.at[pl.ds(0, 15)], hsend).wait()
    pltpu.make_async_copy(wbuf.at[pl.ds(0, 15)], wbuf.at[pl.ds(0, 15)], wsend).wait()
    pltpu.make_async_copy(wbuf.at[pl.ds(0, 16)], wbuf.at[pl.ds(0, 16)], sibsend).wait()
    departed(fresh_in.at[k], K_NEW)
    departed(wq2.at[k], K_WQ)
    departed(wo2.at[k], K_WO)
    departed(tags.at[1], K_TAG_PAIR)
    departed(tags.at[pl.ds(3, 15)], K_TAG)
    departed(opair.at[k, 1 - k], K_OPAIR)
    for t in (0, 1):
        departed(qrecv.at[t, pl.ds(0, 15)], K_Q + t)
        departed(kvrecv.at[t, pl.ds(0, 15)], K_KV + t)
        departed(qpair.at[t, k], K_QPAIR + t)
        departed(states.at[t, k, pl.ds(0, 15)], K_STATE + t)
        departed(states.at[t, k], K_STATEPAIR + t)
    departed(orecv.at[pl.ds(0, 15)], K_OUT)
    departed(frecv.at[pl.ds(0, 15)], K_LAST)
    for copy in outs:
        copy.wait()


def layer(hidden, slot_owner, slot_rows, new_hidden, w_query, w_key, w_value, w_out):
    rows, width = hidden.shape
    cols = w_key.shape[1]
    bf16, f32 = jnp.bfloat16, jnp.float32
    any_ = pl.BlockSpec(memory_space=pl.ANY)
    smem = pl.BlockSpec(memory_space=pltpu.SMEM)
    caches = [jax.ShapeDtypeStruct((rows, cols), bf16)] * 2
    dma = pltpu.SemaphoreType.DMA
    return pl.pallas_call(
        layer_kernel,
        out_shape=caches + [jax.ShapeDtypeStruct((STEPS, 32, 16), bf16)],
        in_specs=[smem, smem] + [any_] * 6,
        out_specs=[any_, any_, pl.BlockSpec(memory_space=pltpu.VMEM)],
        scratch_shapes=[
            pltpu.VMEM((NX * NY, rows, width), bf16),
            pltpu.VMEM((2 * NZ, 2, BLOCK, cols), bf16),
            pltpu.VMEM((2, rows, cols), f32),
            pltpu.VMEM((rows, cols), bf16),
            pltpu.VMEM((rows, cols), bf16),
            pltpu.VMEM((2, STEPS, 2, 16, 256), bf16),
            pltpu.VMEM((2, 256, 256), bf16),
            pltpu.VMEM((2, 256, 256), bf16),
            pltpu.VMEM((STEPS, 16, 256), bf16),
            pltpu.VMEM((STEPS, NZ, 16, 256), bf16),
            pltpu.VMEM((STEPS, 2, 16, 256), bf16),
            pltpu.VMEM((32, 256), f32),
            pltpu.VMEM((STEPS, NZ, 4, 128), f32),
            pltpu.VMEM((STEPS, NZ, 4, 128), f32),
            pltpu.VMEM((STEPS, 4, 128), f32),
            pltpu.VMEM((STEPS, 2, NZ, 8, 128), f32),
            pltpu.VMEM((2, 16, 256), bf16),
            pltpu.VMEM((16, 2, 16, 256), bf16),
            pltpu.VMEM((2, 2, 16, 256), bf16),
            pltpu.VMEM((2, 32, 128), bf16),
            pltpu.VMEM((16, 32, 128), bf16),
            pltpu.VMEM((3 + NZ, 8, 128), f32),
            dma, dma((NX * NY, 4)), dma, dma((2 * NZ, 2)), dma, dma((6,)), dma((2,)),
            dma((KINDS,)), dma((KINDS,)),
        ],
        compiler_params=pltpu.CompilerParams(
            collective_id=0, has_side_effects=True, vmem_limit_bytes=48 << 20
        ),
        name="layer",
    )(
        slot_owner, slot_rows, hidden, new_hidden.reshape(STEPS, 2, 16, 256),
        w_query, w_key, w_value, w_out,
    )


def solution(mesh):
    in_specs = (
        P("cache", "head"),
        P("cache"),
        P("cache"),
        P(None, None, "cache"),
        P("cache", "head"),
        P("cache", "head"),
        P("cache", "head"),
        P("head", "cache"),
    )
    out_specs = (P("cache", "head"), P("cache", "head"), P(None, None, ("cache", "head")))

    def on_device(*arrays):
        return tuple(layer(*arrays))

    return jax.shard_map(
        on_device, mesh=mesh, in_specs=in_specs, out_specs=out_specs, check_vma=False
    )
```

time: 761 us -> 128 us (0.17); the launches traced: 748 us -> 128 us
  blocking collectives: 630 us -> 0 us
  Pallas kernels: 0 us -> 119 us
  waiting for transfers between devices: 43.1 us -> 0 us
  other arithmetic: 22.9 us -> 0 us
  matrix products: 17.1 us -> 0 us
  between operations: 14.6 us -> 0.67 us
  local copies, waits for them, and re-layouts: 18.3 us -> 8.15 us
    unnamed x4 -> x0, blocking collectives: 324 us -> none
    all_gather x11 -> x0, blocking collectives: 306 us -> none  [the longest x6 176 us: joined_2(): lax.all_gather(part.astype(kind), axis)]
    pallas_call x0 -> x1, Pallas kernels: none -> 119 us  [layer(): pl.pallas_call(layer_kernel, out_shape=caches + [jax.ShapeDtypeStruct((ST...]
    all_gather x3 -> x0, waiting for transfers between devices: 41 us -> none  [the longest x1 31.9 us: on_device(): gathered = lax.all_gather(hidden, 'head', axis=1, tiled=True)]
    dot_general x12 -> x0, matrix products: 17.1 us -> none  [the longest x1 6.9 us: on_device(): jnp.dot(gathered, lax.all_gather(w_key, 'cache', axis=0, tiled=True), pre...]
    add x124 -> x0, other arithmetic: 16.1 us -> none  [the longest x62 14.5 us: combine(): accum_one * factor_one[..., None] + accum_two * factor_two[..., None]]
    exp x124 -> x0, local copies, waits for them, and re-layouts: 10.8 us -> none  [the longest x62 5.45 us: combine(): factor_two = jnp.exp(peak_two - peak_both)]
  transfers between devices with their start and end apart: 3 -> 0, of which waited for: 2 -> 0; matrix products, arithmetic and copies ran while one was open for 3% -> 0% of each run, Pallas kernels for 0% -> 0%
where the time goes in v1:
time: 128 us
  Pallas kernels  119 us (93%)
  local copies, waits for them, and re-layouts  8.15 us (6%)
    pallas_call x1, Pallas kernels, layer(): pl.pallas_call(layer_kernel, out_shape=caches + [jax.ShapeDtypeStruct((ST...  119 us
    unnamed x18, local copies, waits for them, and re-layouts  7.47 us

profile of v1, /device:TPU:1, one launch (start us, length us, event | category | flops | bytes accessed | tf_op | source)
XLA Modules:
  0.0 128.0 jit_solution(13726942300646579068)
XLA Ops:
  0.6 0.0 copy-start.7
  0.6 0.0 copy-start.6
  0.7 0.6 copy-done.7
  1.3 0.0 copy-done.6
  1.3 0.0 copy-start
  1.3 1.0 copy-done
  2.3 0.0 copy-start.1
  2.3 0.9 copy-done.1
  3.3 0.0 copy-start.2
  3.3 0.9 copy-done.2
  4.2 0.0 copy-start.3
  4.2 0.9 copy-done.3
  5.1 0.0 copy-start.4
  5.1 0.9 copy-done.4
  6.0 0.0 copy-start.5
  6.0 0.8 copy-done.5
  6.7 119.2 %layer.1 = (bf16[512,256]{1,0:T(8,128)(2,1)S(1)}, bf16[512,256]{1,0:T(8,128)(2,1)S(1)}, bf16[2,32,16]{2,1,0:T(8,128)(2,1)S(1)}) custom-call(s32[2]{0:T(128)S(1)} %copy-done.6, s32[2]{0:T(128)S(1)} %copy-done.7, bf16[512,512]{1,0:T(8,128)(2,1)S(1)} %copy-done, bf16[2,2,16,256]{3,2,1,0:T(8,128)(2,1)S(1)} %bitcast.1, bf16[256,256]{1,0:T(8,128)(2,1)S(1)} %copy-done.1, ...), custom_call_target="tpu_custom_call" | custom-call | tf_op jit(solution)/shard_map/layer/pallas_call | solution.py:508
  125.9 0.7 copy.11
  126.6 0.7 copy.14
  127.3 0.7 copy.15
Async XLA Ops:
  0.6 0.7 copy-start.7
  0.6 0.7 copy-start.6
  1.3 1.0 copy-start
  2.3 0.9 copy-start.1
  3.3 0.9 copy-start.2
  4.2 0.9 copy-start.3
  5.1 0.9 copy-start.4
  6.0 0.8 copy-start.5

commit v2 on v1

v2 whole, which is shorter than its diff:
```python
import jax
import jax.numpy as jnp
from jax import lax
from jax.experimental import pallas as pl
from jax.experimental.pallas import tpu as pltpu
from jax.sharding import PartitionSpec as P

HD = 128
STEPS = 2
MESH = pl.DeviceIdType.MESH
NX, NY, NZ = 4, 4, 16
BLOCK = 256
QUARTER = 128


def place():
    c = lax.axis_index("cache")
    h = lax.axis_index("head")
    return c // 2, lax.rem(c, 2), h // NY, lax.rem(h, NY)


def at(z, k, x, y):
    return {"cache": z * 2 + k, "head": x * NY + y}


def hop(value, by, size):
    return lax.rem(value + (by + size), size)
Z_FAR_FIRST = (8, 7, -7, 6, -6, 5, -5, 4, -4, 3, -3, 2, -2, 1, -1)
PLANE_FAR_FIRST = tuple(
    sorted(
        ((dx, dy) for dx in (2, 1, -1, 0) for dy in (2, 1, -1, 0) if dx or dy),
        key=lambda d: -abs(d[0]) - abs(d[1]),
    )
)
K_NEW, K_WQ, K_WO, K_OPAIR, K_OUT, K_LAST = range(6)
K_Q, K_KV, K_QPAIR, K_STATE, K_STATEPAIR = 6, 8, 10, 12, 14
KINDS = 16
PRODUCT_TICKS = (5, 7, 9, 11, 12, 13, 14, 15)
AHEAD = 3


def layer_kernel(
    owner_ref, rows_ref, hidden_ref, new_ref, wq_ref, wk_ref, wv_ref, wo_ref,
    key_ref, value_ref, out_ref,
    hbuf, wbuf, acc, kout, vout, fresh_in, wq2, wo2,
    qsend, qrecv, qpair, qall, kvsend, kvrecv, kvown, states, osend, orecv, opair, fsend, frecv,
    hsend, hsem, wsend, wsem, sibsend, lsem, osem, msem, mrecv, hellos,
):
    z, k, x, y = place()
    me = x * NY + y
    mine = z * 2 + k
    xn = {s: at(z, k, hop(x, s, NX), y) for s in (1, -1)}
    yn = {s: at(z, k, x, hop(y, s, NY)) for s in (1, -1)}
    zn = {s: at(hop(z, s, NZ), k, x, y) for s in (1, -1)}
    sib = at(z, 1 - k, x, y)
    barrier = pltpu.get_barrier_semaphore()
    partners = [sib, xn[1], xn[-1], yn[1], yn[-1], zn[1], zn[-1]]
    for other in partners:
        pl.semaphore_signal(barrier, inc=1, device_id=other, device_id_type=MESH)
    local = [
        pltpu.make_async_copy(hidden_ref, hbuf.at[me], lsem.at[0]),
        pltpu.make_async_copy(wk_ref, wbuf.at[mine, 0], lsem.at[1]),
        pltpu.make_async_copy(wv_ref, wbuf.at[mine, 1], lsem.at[2]),
        pltpu.make_async_copy(new_ref, fresh_in.at[k], lsem.at[3]),
        pltpu.make_async_copy(wq_ref, wq2.at[k], lsem.at[4]),
        pltpu.make_async_copy(wo_ref, wo2.at[k], lsem.at[5]),
    ]
    for copy in local:
        copy.start()
    pl.semaphore_wait(barrier, len(partners))

    def source(dx, dy):
        return hop(x, dx, NX) * NY + hop(y, dy, NY)

    def push(dx, dy, piece, to, own=False):
        index = source(dx, dy)
        rows = pl.ds(piece * QUARTER, QUARTER)
        src = hidden_ref.at[rows] if own else hbuf.at[index, rows]
        pltpu.make_async_remote_copy(
            src_ref=src, dst_ref=hbuf.at[index, rows],
            send_sem=hsend, recv_sem=hsem.at[index, piece],
            device_id=to, device_id_type=MESH,
        ).start()

    def landed(dx, dy, pieces):
        index = source(dx, dy)
        for piece in pieces:
            part = hbuf.at[index, pl.ds(piece * QUARTER, QUARTER)]
            pltpu.make_async_copy(part, part, hsem.at[index, piece]).wait()

    def piece_of(half, sign, turn):
        return 2 * half + (turn if sign == 1 else 1 - turn)

    SLOTS = {
        1: ("own", 0, 0), 2: ("own", 0, 1), 3: ("own", 1, 0), 4: ("own", 1, 1), 5: ("pass", 0, 0),
        6: (-1, 1, 0), 7: (-1, 1, 1), 8: (1, 1, 0), 9: (1, 1, 1), 10: ("pass", 1, 0),
        11: (2, 1, 0), 12: (2, 1, 1), 13: ("pass", 1, -1), 14: ("pass", 1, 1), 15: ("pass", 1, 2),
    }

    def hidden_slot(slot, arriving):
        what, axis, turn = SLOTS[slot]
        for half in (0, 1):
            nb = xn if axis == half else yn
            for sign in (1, -1):
                if what == "pass":
                    a, b = (-sign, 0) if axis == 0 else (turn, -sign)
                    piece = piece_of(half, sign, 0)
                    if arriving:
                        a, b = (2, 0) if axis == 0 else (turn, 2)
                else:
                    a, b = (0, 0) if what == "own" else (what, 0)
                    piece = piece_of(half, sign, turn)
                    if arriving:
                        a, b = (-sign, b) if axis == 0 else (a, -sign)
                dx, dy = (a, b) if half == 0 else (b, a)
                if arriving:
                    landed(dx, dy, (piece,))
                else:
                    push(dx, dy, piece, nb[sign], own=what == "own")

    def ready(dx, dy):
        ax, ay = jnp.minimum(dx, NX - dx), jnp.minimum(dy, NY - dy)
        near = ax + ay
        side = jnp.where((dx == 3) | (dy == 3), 13, 14)
        both = jnp.where((dx == 3) & (dy == 3), 7, 9)
        straight = jnp.where(near == 1, 4, 10)
        far = jnp.where(near == 4, 15, side)
        out = jnp.where(near == 2, both, far)
        out = jnp.where((ax == 0) | (ay == 0), straight, out)
        return jnp.where(near == 0, 0, out)

    def block(dz, core):
        return hop(z, dz, NZ) * 2 + core

    def ring(dz, chunk, part, to):
        rows = pl.ds(part * QUARTER, QUARTER)
        held = wbuf.at[block(dz, k), chunk, rows]
        src = (wk_ref if chunk == 0 else wv_ref).at[rows] if dz == 0 else held
        pltpu.make_async_remote_copy(
            src_ref=src, dst_ref=held, send_sem=wsend,
            recv_sem=wsem.at[block(dz, k), chunk, part],
            device_id=to, device_id_type=MESH,
        ).start()

    def share(dz, chunk):
        part = wbuf.at[block(dz, k), chunk]
        src = (wk_ref if chunk == 0 else wv_ref) if dz == 0 else part
        pltpu.make_async_remote_copy(
            src_ref=src, dst_ref=part, send_sem=sibsend, recv_sem=wsem.at[block(dz, k), chunk, 0],
            device_id=sib, device_id_type=MESH,
        ).start()

    def have(dz, core, chunk):
        part = wbuf.at[block(dz, core), chunk]
        pltpu.make_async_copy(part, part, wsem.at[block(dz, core), chunk, 0]).wait()

    def have_part(dz, chunk, part):
        held = wbuf.at[block(dz, k), chunk, pl.ds(part * QUARTER, QUARTER)]
        pltpu.make_async_copy(held, held, wsem.at[block(dz, k), chunk, part]).wait()

    def weight_slot(slot):
        r, chunk, part = (slot + 3) // 4, (slot - 1) % 4 // 2, (slot - 1) % 2
        if r < NZ // 2:
            for sign in (1, -1):
                have_part(-sign * r, chunk, part)
                if r < NZ // 2 - 1 or (sign == 1) == (chunk == 0):
                    ring(-sign * r, chunk, part, zn[sign])
        else:
            for chunk in (0, 1):
                have_part(NZ // 2, chunk, part)

    def hello(step):
        for side, sign in ((0, 1), (1, -1)):
            pl.semaphore_signal(hellos.at[side], inc=1, device_id=zn[sign], device_id_type=MESH)
        for side in (0, 1):
            pl.semaphore_wait(hellos.at[side], 1)

    def share_tick(tick):
        if tick == 0:
            for chunk in (0, 1):
                share(0, chunk)
        elif tick < NZ - 1:
            for sign in (1, -1):
                share(-sign * ((tick + 1) // 2), (tick + 1) % 2)
        else:
            for chunk in (0, 1):
                share(NZ // 2, chunk)

    def weight_settle(r):
        for dz in ((r, -r) if 0 < r < NZ // 2 else (r,)):
            for chunk in (0, 1):
                have(dz, 1 - k, chunk)

    def products(after, upto):
        def one(h, carry):
            due = ready(hop(h // NY, NX - x, NX), hop(lax.rem(h, NY), NY - y, NY))
            away = hop(h, NZ - z, NZ)
            due = jnp.maximum(due, jnp.minimum(2 * jnp.minimum(away, NZ - away), NZ - 1))
            now = (due > after) & (due <= upto)

            @pl.when(now)
            def _():
                for chunk in (0, 1):
                    part = jnp.dot(
                        hbuf[h, :, :BLOCK], wbuf[2 * h, chunk], preferred_element_type=jnp.float32
                    ) + jnp.dot(
                        hbuf[h, :, BLOCK:], wbuf[2 * h + 1, chunk], preferred_element_type=jnp.float32
                    )
                    acc[chunk] += part

            return carry

        lax.fori_loop(0, NX * NY, one, 0)

    def remote(src, dst, kind, to):
        pltpu.make_async_remote_copy(
            src_ref=src, dst_ref=dst, send_sem=msem.at[kind], recv_sem=mrecv.at[kind],
            device_id=to, device_id_type=MESH,
        ).start()

    def arrived(part, kind):
        pltpu.make_async_copy(part, part, mrecv.at[kind]).wait()

    def departed(part, kind):
        pltpu.make_async_copy(part, part, msem.at[kind]).wait()

    def along_z(src, dst, kind, part=slice(None)):
        for dz in Z_FAR_FIRST[part]:
            remote(src, dst, kind, at(hop(z, dz, NZ), k, x, y))

    lane = lax.broadcasted_iota(jnp.int32, (1, 128), 1)

    def tag_row(values):
        row = jnp.zeros((1, 128), jnp.float32)
        for r, value in enumerate(values):
            row = jnp.where(lane == z * 8 + r, value, row)
        return row

    def pair_start():
        remote(new_ref, fresh_in.at[k], K_NEW, sib)
        remote(wq_ref, wq2.at[k], K_WQ, sib)
        remote(wo_ref, wo2.at[k], K_WO, sib)

    def pair_finish():
        arrived(fresh_in.at[k], K_NEW)
        arrived(wq2.at[k], K_WQ)
        arrived(wo2.at[k], K_WO)

    def project_query(t, tokens):
        q = jnp.zeros((16, 256), jnp.float32)
        for core in (0, 1):
            q += jnp.dot(tokens[core], wq2[core], preferred_element_type=jnp.float32)
        q16 = q.astype(jnp.bfloat16)
        qsend[t] = q16
        qrecv[t, z] = q16

    def send_query(t, part=slice(None)):
        along_z(qsend.at[t], qrecv.at[t, z], K_Q + t, part)

    def project_new(t, tokens):
        for chunk in (0, 1):
            kv = jnp.zeros((16, 256), jnp.float32)
            for core in (0, 1):
                kv += jnp.dot(
                    tokens[core], wbuf[2 * z + core, chunk], preferred_element_type=jnp.float32
                )
            for j in (0, 1):
                kvsend[t, :, 2 * chunk + j, :] = kv[:, j * HD : (j + 1) * HD]

    def send_new(t, part=slice(None)):
        rows = pl.ds(0, 6 if t == 0 else 4)
        for dz in Z_FAR_FIRST[part]:
            to = hop(z, dz, NZ)
            remote(kvsend.at[t, to, rows], kvrecv.at[t, z, rows], K_KV + t, at(to, k, x, y))

    def project_first():
        tokens = [fresh_in[0, 0, k], fresh_in[1, 0, k]]
        project_new(0, tokens)
        q = jnp.zeros((16, 256), jnp.float32)
        for core in (0, 1):
            q += jnp.dot(tokens[core], wq2[core], preferred_element_type=jnp.float32)
        for j in (0, 1):
            kvsend[0, :, 4 + j, :] = q[:, j * HD : (j + 1) * HD]

    def query_first():
        new_pair(0)
        along_z(qall.at[k * 16 + z], qall.at[k * 16 + z], K_Q)

    def query_first_half():
        arrived(qall.at[pl.ds(0, 15)], K_Q)
        half = qall.at[pl.ds(k * 16, 16)]
        remote(half, half, K_QPAIR, sib)

    def query_first_rest():
        arrived(qall.at[pl.ds(0, 16)], K_QPAIR)

    def query_half(t):
        arrived(qrecv.at[t, pl.ds(0, 15)], K_Q + t)
        half = jnp.sum(qrecv[t].astype(jnp.float32), axis=0).astype(jnp.bfloat16)
        qpair[t, k] = half
        remote(qpair.at[t, k], qpair.at[t, k], K_QPAIR + t, sib)
        return half.astype(jnp.float32)

    def query_rest(t):
        arrived(qpair.at[t, 1 - k], K_QPAIR + t)
        for half in (0, 1):
            q = qpair[t, half].astype(jnp.float32)
            for j in (0, 1):
                qall[16 * half : 16 * half + 16, j, :] = q[:, j * HD : (j + 1) * HD]

    def new_pair(t):
        rows = 6 if t == 0 else 4
        kvrecv[t, z] = kvsend[t, z]
        arrived(kvrecv.at[t, pl.ds(0, 15), pl.ds(0, rows)], K_KV + t)
        total = jnp.sum(kvrecv[t, :, 0:rows, :], axis=0).astype(jnp.bfloat16).astype(jnp.float32)
        kvown[t] = total[0:4]
        if t == 0:
            qall[k * 16 + z] = total[4:6]

    scale = HD ** (-0.5)
    sub2 = lax.broadcasted_iota(jnp.int32, (2, 128), 0)

    def new_state(t):
        q2 = qall[k * 16 + z]
        scores = [
            jnp.sum(q2 * kvown[s, 0:2, :], axis=1, keepdims=True) * scale for s in range(t + 1)
        ]
        peak = scores[0]
        for s in scores[1:]:
            peak = jnp.maximum(peak, s)
        mass = jnp.zeros((2, 1), jnp.float32)
        mixed = jnp.zeros((2, HD), jnp.float32)
        for s, score in enumerate(scores):
            w = jnp.exp(score - peak)
            mass += w
            mixed += w * kvown[s, 2:4, :]
        return mixed / mass, peak + jnp.log(mass)

    def slot_state(i):
        rows = pl.ds(i * BLOCK, BLOCK)
        q = qall[owner_ref[i]]
        spot = lax.broadcasted_iota(jnp.int32, (8, 256), 1)
        line = lax.broadcasted_iota(jnp.int32, (8, 128), 0)
        q2 = jnp.concatenate(
            [jnp.where(line == j, q[j : j + 1], 0.0).astype(jnp.bfloat16) for j in (0, 1)], axis=1
        )
        scores = lax.dot_general(
            q2, kout[rows, :], (((1,), (1,)), ((), ())), preferred_element_type=jnp.float32
        )
        scores = jnp.where(spot < rows_ref[i], scores * scale, -1e30)
        peak = jnp.max(scores, axis=1, keepdims=True)
        w = jnp.exp(scores - peak)
        mass = jnp.sum(w, axis=1, keepdims=True)
        mixed = jnp.dot(w.astype(jnp.bfloat16), vout[rows, :], preferred_element_type=jnp.float32)
        mixed = mixed / mass
        lse = peak + jnp.log(mass)
        return jnp.where(sub2 == 0, mixed[0:2, :HD], mixed[0:2, HD:]), lse[0:2]

    def exchange_states(t):
        tag = []
        for i in range(3):
            mixed, lse = slot_state(i) if i < 2 else new_state(t)
            states[t, k, z, 2 * i : 2 * i + 2, :] = mixed
            tag += [lse[0:1], lse[1:2]]
        states[t, k, z, 6:7, :] = tag_row(tag)
        first, second = owner_ref[0].astype(jnp.float32), owner_ref[1].astype(jnp.float32)
        own = (k * 16 + z).astype(jnp.float32)
        states[t, k, z, 7:8, :] = tag_row([first, first, second, second, own, own, -1.0, -1.0])
        along_z(states.at[t, k, z], states.at[t, k, z], K_STATE + t)
        arrived(states.at[t, k, pl.ds(0, 15)], K_STATE + t)
        remote(states.at[t, k], states.at[t, k], K_STATEPAIR + t, sib)
        arrived(states.at[t, 1 - k], K_STATEPAIR + t)

    def attention(t, first, count):
        held = states[t].reshape(256, 128)
        total = [jnp.sum(states[t, core], axis=0) for core in (0, 1)]
        lse = jnp.concatenate([total[0][6:7], total[1][6:7]], axis=1)
        owner = jnp.concatenate([total[0][7:8], total[1][7:8]], axis=1)
        spot = lax.broadcasted_iota(jnp.int32, (count, 256), 1)
        conv = (lax.broadcasted_iota(jnp.int32, (count, 256), 0) + first).astype(jnp.float32)
        mine_ = owner == conv
        held = held.astype(jnp.bfloat16)
        parts = []
        for j in (0, 1):
            valid = mine_ & (lax.rem(spot, 2) == j)
            kept = jnp.where(valid, lse, -1e30)
            peak = jnp.max(kept, axis=1, keepdims=True)
            w = jnp.where(valid, jnp.exp(kept - peak), 0.0)
            w = w / jnp.sum(w, axis=1, keepdims=True)
            parts.append(
                jnp.dot(w.astype(jnp.bfloat16), held, preferred_element_type=jnp.float32)
            )
        return jnp.concatenate(parts, axis=1).astype(jnp.bfloat16)

    def plane(pick, dst, kind):
        for dx, dy in PLANE_FAR_FIRST:
            to = source(dx, dy)
            remote(pick(to), dst, kind, at(z, k, hop(x, dx, NX), hop(y, dy, NY)))

    def next_tokens():
        half = attention(0, 16 * k, 16)
        for core in (0, 1):
            part = jnp.dot(half, wo2[core], preferred_element_type=jnp.float32).astype(jnp.bfloat16)
            osend[core] = part
            orecv[me, core] = part
        plane(lambda to: osend, orecv.at[me], K_OUT)
        arrived(orecv.at[pl.ds(0, 15)], K_OUT)
        tokens = []
        for core in (0, 1):
            out = jnp.sum(orecv[:, core].astype(jnp.float32), axis=0).astype(jnp.bfloat16)
            opair[k, core] = out
            tokens.append(
                (fresh_in[core, 1, k].astype(jnp.float32) + out.astype(jnp.float32)).astype(
                    jnp.bfloat16
                )
            )
        return tokens

    def own_columns(value, width, start):
        pick = lax.broadcasted_iota(jnp.int32, (width, 16), 0) == (
            lax.broadcasted_iota(jnp.int32, (width, 16), 1) + start
        )
        return jnp.dot(
            value, pick.astype(jnp.bfloat16), preferred_element_type=jnp.float32
        ).astype(jnp.bfloat16)

    def last_output():
        both = attention(1, 0, 32)
        part = jnp.dot(both, wo2[k], preferred_element_type=jnp.float32).astype(jnp.bfloat16)
        for side in (0, 1):
            fsend[side] = part[:, side * 128 : (side + 1) * 128]
        frecv[me] = fsend[me // 8]
        plane(lambda to: fsend.at[to // 8], frecv.at[me], K_LAST)
        for half in (0, 1):
            out_ref[0, 16 * half : 16 * half + 16, :] = own_columns(opair[half, k], 256, me * 16)
        arrived(frecv.at[pl.ds(0, 15)], K_LAST)
        out = jnp.sum(frecv[...].astype(jnp.float32), axis=0).astype(jnp.bfloat16)
        out_ref[1] = own_columns(out, 128, lax.rem(me, 8) * 16)

    for chunk in (0, 1):
        acc[chunk] = jnp.zeros(acc.shape[1:], jnp.float32)
    settled = -1
    done = -1
    near, rest = slice(0, 8), slice(8, None)
    for tick in range(NZ):
        if tick == 0:
            for chunk in (0, 1):
                for part in (0, 1):
                    for sign in (1, -1):
                        ring(0, chunk, part, zn[sign])
                hidden_slot(1 + chunk, False)
            hidden_slot(3, False)
            share_tick(0)
            pair_start()
        else:
            weight_slot(2 * tick - 1)
            if tick <= 4:
                hello(2 * tick - 1)
            hidden_slot(tick, True)
            if tick + AHEAD < NZ:
                hidden_slot(tick + AHEAD, False)
            weight_slot(2 * tick)
            if tick <= 4:
                hello(2 * tick)
            share_tick(tick)
        if tick == 2:
            for copy in local:
                copy.wait()
            pair_finish()
            weight_settle(0)
            settled = 0
            project_first()
        if tick == 4:
            send_new(0, near)
        if tick == 5:
            send_new(0, rest)
        if tick == 9:
            query_first()
        if tick == 12:
            query_first_half()
        if tick == 13:
            query_first_rest()
        if tick in PRODUCT_TICKS:
            upto = tick if tick == NZ - 1 else tick - 1
            while settled < NZ // 2 and min(2 * (settled + 1), NZ - 1) <= upto:
                settled += 1
                weight_settle(settled)
            products(done, upto)
            done = upto
    for slot in (0, 1):
        rows = pl.ds(slot * BLOCK, BLOCK)
        keep = lax.broadcasted_iota(jnp.int32, (BLOCK, BLOCK), 0) < rows_ref[slot]
        for chunk, out in ((0, kout), (1, vout)):
            out[rows, :] = jnp.where(keep, acc[chunk, rows, :], 0.0).astype(jnp.bfloat16)
    outs = [
        pltpu.make_async_copy(kout, key_ref, osem.at[0]),
        pltpu.make_async_copy(vout, value_ref, osem.at[1]),
    ]
    for copy in outs:
        copy.start()
    exchange_states(0)
    tokens = next_tokens()
    project_query(1, tokens)
    send_query(1)
    project_new(1, tokens)
    send_new(1)
    remote(opair.at[k, 1 - k], opair.at[k, 1 - k], K_OPAIR, sib)
    query_half(1)
    new_pair(1)
    departed(qall.at[pl.ds(0, 15)], K_Q)
    departed(qall.at[pl.ds(0, 16)], K_QPAIR)
    query_rest(1)
    exchange_states(1)
    arrived(opair.at[1 - k, k], K_OPAIR)
    last_output()

    pltpu.make_async_copy(hbuf.at[pl.ds(0, 15)], hbuf.at[pl.ds(0, 15)], hsend).wait()
    pltpu.make_async_copy(wbuf.at[pl.ds(0, 15)], wbuf.at[pl.ds(0, 15)], wsend).wait()
    pltpu.make_async_copy(wbuf.at[pl.ds(0, 16)], wbuf.at[pl.ds(0, 16)], sibsend).wait()
    departed(fresh_in.at[k], K_NEW)
    departed(wq2.at[k], K_WQ)
    departed(wo2.at[k], K_WO)
    departed(opair.at[k, 1 - k], K_OPAIR)
    departed(kvrecv.at[0, pl.ds(0, 15), pl.ds(0, 6)], K_KV)
    departed(qrecv.at[1, pl.ds(0, 15)], K_Q + 1)
    departed(kvrecv.at[1, pl.ds(0, 15), pl.ds(0, 4)], K_KV + 1)
    departed(qpair.at[1, k], K_QPAIR + 1)
    for t in (0, 1):
        departed(states.at[t, k, pl.ds(0, 15)], K_STATE + t)
        departed(states.at[t, k], K_STATEPAIR + t)
    departed(orecv.at[pl.ds(0, 15)], K_OUT)
    departed(frecv.at[pl.ds(0, 15)], K_LAST)
    for copy in outs:
        copy.wait()


def layer(hidden, slot_owner, slot_rows, new_hidden, w_query, w_key, w_value, w_out):
    rows, width = hidden.shape
    cols = w_key.shape[1]
    bf16, f32 = jnp.bfloat16, jnp.float32
    any_ = pl.BlockSpec(memory_space=pl.ANY)
    hbm = pl.BlockSpec(memory_space=pltpu.HBM)
    smem = pl.BlockSpec(memory_space=pltpu.SMEM)
    caches = [jax.ShapeDtypeStruct((rows, cols), bf16)] * 2
    dma = pltpu.SemaphoreType.DMA
    return pl.pallas_call(
        layer_kernel,
        out_shape=caches + [jax.ShapeDtypeStruct((STEPS, 32, 16), bf16)],
        in_specs=[smem, smem] + [hbm] * 6,
        out_specs=[any_, any_, pl.BlockSpec(memory_space=pltpu.VMEM)],
        scratch_shapes=[
            pltpu.VMEM((NX * NY, rows, width), bf16),
            pltpu.VMEM((2 * NZ, 2, BLOCK, cols), bf16),
            pltpu.VMEM((2, rows, cols), f32),
            pltpu.VMEM((rows, cols), bf16),
            pltpu.VMEM((rows, cols), bf16),
            pltpu.VMEM((2, STEPS, 2, 16, 256), bf16),
            pltpu.VMEM((2, 256, 256), bf16),
            pltpu.VMEM((2, 256, 256), bf16),
            pltpu.VMEM((STEPS, 16, 256), bf16),
            pltpu.VMEM((STEPS, NZ, 16, 256), bf16),
            pltpu.VMEM((STEPS, 2, 16, 256), bf16),
            pltpu.VMEM((32, 2, 128), f32),
            pltpu.VMEM((STEPS, NZ, 8, 128), f32),
            pltpu.VMEM((STEPS, NZ, 8, 128), f32),
            pltpu.VMEM((STEPS, 4, 128), f32),
            pltpu.VMEM((STEPS, 2, NZ, 8, 128), f32),
            pltpu.VMEM((2, 16, 256), bf16),
            pltpu.VMEM((16, 2, 16, 256), bf16),
            pltpu.VMEM((2, 2, 16, 256), bf16),
            pltpu.VMEM((2, 32, 128), bf16),
            pltpu.VMEM((16, 32, 128), bf16),
            dma, dma((NX * NY, 4)), dma, dma((2 * NZ, 2, 2)), dma, dma((6,)), dma((2,)),
            dma((KINDS,)), dma((KINDS,)), pltpu.SemaphoreType.REGULAR((2,)),
        ],
        compiler_params=pltpu.CompilerParams(
            collective_id=0, has_side_effects=True, vmem_limit_bytes=60 << 20
        ),
        name="layer",
    )(
        slot_owner, slot_rows, hidden, new_hidden.reshape(STEPS, 2, 16, 256),
        w_query, w_key, w_value, w_out,
    )


def solution(mesh):
    in_specs = (
        P("cache", "head"),
        P("cache"),
        P("cache"),
        P(None, None, "cache"),
        P("cache", "head"),
        P("cache", "head"),
        P("cache", "head"),
        P("head", "cache"),
    )
    out_specs = (P("cache", "head"), P("cache", "head"), P(None, None, ("cache", "head")))

    def on_device(*arrays):
        return tuple(layer(*arrays))

    return jax.shard_map(
        on_device, mesh=mesh, in_specs=in_specs, out_specs=out_specs, check_vma=False
    )
```

time: 128 us -> 115 us (0.90)
  Pallas kernels: 119 us -> 110 us
  local copies, waits for them, and re-layouts: 8.15 us -> 3.81 us
    pallas_call x1, Pallas kernels: 119 us -> 110 us  [layer(): pl.pallas_call(layer_kernel, out_shape=caches + [jax.ShapeDtypeStruct((ST...]
    unnamed x18 -> x4, local copies, waits for them, and re-layouts: 7.47 us -> 2.42 us
where the time goes in v2:
time: 115 us; the launch traced here: 114 us
  Pallas kernels  110 us (96%)
  local copies, waits for them, and re-layouts  3.81 us (3%)
    pallas_call x1, Pallas kernels, layer(): pl.pallas_call(layer_kernel, out_shape=caches + [jax.ShapeDtypeStruct((ST...  110 us
    unnamed x4, local copies, waits for them, and re-layouts  2.42 us

profile of v2, /device:TPU:1, one launch (start us, length us, event | category | flops | bytes accessed | tf_op | source)
XLA Modules:
  0.0 114.3 jit_solution(1200104444848830399)
XLA Ops:
  0.6 109.9 %layer.1 = (bf16[512,256]{1,0:T(8,128)(2,1)}, bf16[512,256]{1,0:T(8,128)(2,1)}, bf16[2,32,16]{2,1,0:T(8,128)(2,1)}) custom-call(s32[2]{0:T(128)} %owner_ref.1, s32[2]{0:T(128)} %rows_ref.1, bf16[512,512]{1,0:T(8,128)(2,1)} %hidden_ref.1, bf16[2,2,16,256]{3,2,1,0:T(8,128)(2,1)} %bitcast.1, bf16[256,256]{1,0:T(8,128)(2,1)} %wq_ref.1, bf16[256,256]{1,0:T(8,128)(2,1)} %wk_ref.1, ...), custom_call_target="tpu_custom_call" | custom-call | tf_op jit(solution)/shard_map/layer/pallas_call | solution.py:546
  110.5 1.4 %copy.11 = bf16[2,32,16]{1,2,0:T(8,128)(2,1)} copy(bf16[2,32,16]{2,1,0:T(8,128)(2,1)} %get-tuple-element.5) | data formatting | bytes 4096 | tf_op jit(solution)/shard_map/layer/pallas_call | solution.py:546
  111.9 0.0 copy-start
  111.9 1.7 %copy.14 = bf16[512,256]{1,0:T(8,128)(2,1)} copy(bf16[512,256]{1,0:T(8,128)(2,1)} %get-tuple-element.9) | data formatting | bytes 524288
  113.6 0.0 copy-done
  113.6 0.7 copy.15
Async XLA Ops:
  111.9 1.7 %copy-start = (bf16[512,256]{1,0:T(8,128)(2,1)S(1)}, bf16[512,256]{1,0:T(8,128)(2,1)}, u32[]{:S(2)}) copy-start(bf16[512,256]{1,0:T(8,128)(2,1)} %get-tuple-element.10) | copy-start | bytes 786436

commit v3 on v2

--- a/solution.py
+++ b/solution.py
@@ -35,7 +35,7 @@
 K_NEW, K_WQ, K_WO, K_OPAIR, K_OUT, K_LAST = range(6)
 K_Q, K_KV, K_QPAIR, K_STATE, K_STATEPAIR = 6, 8, 10, 12, 14
 KINDS = 16
-PRODUCT_TICKS = (5, 7, 9, 11, 12, 13, 14, 15)
+PRODUCT_TICKS = (5, 7, 9, 11, 12, 13, 14)
 AHEAD = 3
 
 
@@ -142,11 +142,14 @@
             device_id=to, device_id_type=MESH,
         ).start()
 
-    def share(dz, chunk):
-        part = wbuf.at[block(dz, k), chunk]
-        src = (wk_ref if chunk == 0 else wv_ref) if dz == 0 else part
+    def share(dz, chunk, part=None):
+        held, sem = wbuf.at[block(dz, k), chunk], wsem.at[block(dz, k), chunk, part or 0]
+        src = (wk_ref if chunk == 0 else wv_ref) if dz == 0 else held
+        if part is not None:
+            held = held.at[pl.ds(part * QUARTER, QUARTER)]
+            src = held
         pltpu.make_async_remote_copy(
-            src_ref=src, dst_ref=part, send_sem=sibsend, recv_sem=wsem.at[block(dz, k), chunk, 0],
+            src_ref=src, dst_ref=held, send_sem=sibsend, recv_sem=sem,
             device_id=sib, device_id_type=MESH,
         ).start()
 
@@ -154,9 +157,9 @@
         part = wbuf.at[block(dz, core), chunk]
         pltpu.make_async_copy(part, part, wsem.at[block(dz, core), chunk, 0]).wait()
 
-    def have_part(dz, chunk, part):
-        held = wbuf.at[block(dz, k), chunk, pl.ds(part * QUARTER, QUARTER)]
-        pltpu.make_async_copy(held, held, wsem.at[block(dz, k), chunk, part]).wait()
+    def have_part(dz, chunk, part, core=k):
+        held = wbuf.at[block(dz, core), chunk, pl.ds(part * QUARTER, QUARTER)]
+        pltpu.make_async_copy(held, held, wsem.at[block(dz, core), chunk, part]).wait()
 
     def weight_slot(slot):
         r, chunk, part = (slot + 3) // 4, (slot - 1) % 4 // 2, (slot - 1) % 2
@@ -168,10 +171,13 @@
         else:
             for chunk in (0, 1):
                 have_part(NZ // 2, chunk, part)
-
-    def hello(step):
+                share(NZ // 2, chunk, part)
+
+    def hello():
         for side, sign in ((0, 1), (1, -1)):
             pl.semaphore_signal(hellos.at[side], inc=1, device_id=zn[sign], device_id_type=MESH)
+
+    def heard():
         for side in (0, 1):
             pl.semaphore_wait(hellos.at[side], 1)
 
@@ -182,14 +188,42 @@
         elif tick < NZ - 1:
             for sign in (1, -1):
                 share(-sign * ((tick + 1) // 2), (tick + 1) % 2)
-        else:
-            for chunk in (0, 1):
-                share(NZ // 2, chunk)
 
     def weight_settle(r):
         for dz in ((r, -r) if 0 < r < NZ // 2 else (r,)):
             for chunk in (0, 1):
                 have(dz, 1 - k, chunk)
+
+    def add(h, cores):
+        for chunk in (0, 1):
+            part = None
+            for core in cores:
+                term = jnp.dot(
+                    hbuf[h, :, pl.ds(core * BLOCK, BLOCK)], wbuf[2 * h + core, chunk],
+                    preferred_element_type=jnp.float32,
+                )
+                part = term if part is None else part + term
+            acc[chunk] += part
+
+    def last_products():
+        corner, across = source(2, 2), hop(z, NZ // 2, NZ)
+
+        @pl.when(corner != across)
+        def _():
+            add(corner, (0, 1))
+
+        for core in (0, 1):
+            @pl.when(k == core)
+            def _():
+                add(across, (core,))
+
+        for part in (0, 1):
+            for chunk in (0, 1):
+                have_part(NZ // 2, chunk, part, 1 - k)
+        for core in (0, 1):
+            @pl.when(k != core)
+            def _():
+                add(across, (core,))
 
     def products(after, upto):
         def one(h, carry):
@@ -200,13 +234,7 @@
 
             @pl.when(now)
             def _():
-                for chunk in (0, 1):
-                    part = jnp.dot(
-                        hbuf[h, :, :BLOCK], wbuf[2 * h, chunk], preferred_element_type=jnp.float32
-                    ) + jnp.dot(
-                        hbuf[h, :, BLOCK:], wbuf[2 * h + 1, chunk], preferred_element_type=jnp.float32
-                    )
-                    acc[chunk] += part
+                add(h, (0, 1))
 
             return carry
 
@@ -224,9 +252,16 @@
     def departed(part, kind):
         pltpu.make_async_copy(part, part, msem.at[kind]).wait()
 
-    def along_z(src, dst, kind, part=slice(None)):
-        for dz in Z_FAR_FIRST[part]:
-            remote(src, dst, kind, at(hop(z, dz, NZ), k, x, y))
+    def each_z(send):
+        def one(i, carry):
+            d = NZ // 2 - (i + 1) // 2
+            send(hop(z, jnp.where(lax.rem(i, 2) == 1, d, -d), NZ))
+            return carry
+
+        lax.fori_loop(0, NZ - 1, one, 0)
+
+    def along_z(src, dst, kind):
+        each_z(lambda to: remote(src, dst, kind, at(to, k, x, y)))
 
     lane = lax.broadcasted_iota(jnp.int32, (1, 128), 1)
 
@@ -254,8 +289,8 @@
         qsend[t] = q16
         qrecv[t, z] = q16
 
-    def send_query(t, part=slice(None)):
-        along_z(qsend.at[t], qrecv.at[t, z], K_Q + t, part)
+    def send_query(t):
+        along_z(qsend.at[t], qrecv.at[t, z], K_Q + t)
 
     def project_new(t, tokens):
         for chunk in (0, 1):
@@ -267,11 +302,17 @@
             for j in (0, 1):
                 kvsend[t, :, 2 * chunk + j, :] = kv[:, j * HD : (j + 1) * HD]
 
-    def send_new(t, part=slice(None)):
+    def send_new(t, offsets=None):
         rows = pl.ds(0, 6 if t == 0 else 4)
-        for dz in Z_FAR_FIRST[part]:
-            to = hop(z, dz, NZ)
+
+        def send(to):
             remote(kvsend.at[t, to, rows], kvrecv.at[t, z, rows], K_KV + t, at(to, k, x, y))
+
+        if offsets is None:
+            each_z(send)
+        else:
+            for dz in offsets:
+                send(hop(z, dz, NZ))
 
     def project_first():
         tokens = [fresh_in[0, 0, k], fresh_in[1, 0, k]]
@@ -393,9 +434,17 @@
         return jnp.concatenate(parts, axis=1).astype(jnp.bfloat16)
 
     def plane(pick, dst, kind):
-        for dx, dy in PLANE_FAR_FIRST:
-            to = source(dx, dy)
-            remote(pick(to), dst, kind, at(z, k, hop(x, dx, NX), hop(y, dy, NY)))
+        def one(i, carry):
+            dx, dy = 2 - i // NY, 2 - lax.rem(i, NY)
+            to = hop(x, dx, NX) * NY + hop(y, dy, NY)
+
+            @pl.when(to != me)
+            def _():
+                remote(pick(to), dst, kind, at(z, k, to // NY, lax.rem(to, NY)))
+
+            return carry
+
+        lax.fori_loop(0, NX * NY, one, 0)
 
     def next_tokens():
         half = attention(0, 16 * k, 16)
@@ -417,11 +466,12 @@
         return tokens
 
     def own_columns(value, width, start):
-        pick = lax.broadcasted_iota(jnp.int32, (width, 16), 0) == (
-            lax.broadcasted_iota(jnp.int32, (width, 16), 1) + start
+        pick = lax.broadcasted_iota(jnp.int32, (16, width), 1) == (
+            lax.broadcasted_iota(jnp.int32, (16, width), 0) + start
         )
-        return jnp.dot(
-            value, pick.astype(jnp.bfloat16), preferred_element_type=jnp.float32
+        return lax.dot_general(
+            pick.astype(jnp.bfloat16), value, (((1,), (1,)), ((), ())),
+            preferred_element_type=jnp.float32,
         ).astype(jnp.bfloat16)
 
     def last_output():
@@ -431,8 +481,9 @@
             fsend[side] = part[:, side * 128 : (side + 1) * 128]
         frecv[me] = fsend[me // 8]
         plane(lambda to: fsend.at[to // 8], frecv.at[me], K_LAST)
-        for half in (0, 1):
-            out_ref[0, 16 * half : 16 * half + 16, :] = own_columns(opair[half, k], 256, me * 16)
+        out_ref[0] = own_columns(
+            jnp.concatenate([opair[0, k], opair[1, k]], axis=0), 256, me * 16
+        )
         arrived(frecv.at[pl.ds(0, 15)], K_LAST)
         out = jnp.sum(frecv[...].astype(jnp.float32), axis=0).astype(jnp.bfloat16)
         out_ref[1] = own_columns(out, 128, lax.rem(me, 8) * 16)
@@ -441,7 +492,6 @@
         acc[chunk] = jnp.zeros(acc.shape[1:], jnp.float32)
     settled = -1
     done = -1
-    near, rest = slice(0, 8), slice(8, None)
     for tick in range(NZ):
         if tick == 0:
             for chunk in (0, 1):
@@ -453,15 +503,20 @@
             share_tick(0)
             pair_start()
         else:
+            if tick == NZ - 1:
+                settled += 1
+                weight_settle(settled)
+                products(done, tick - 1)
+                done = tick - 1
             weight_slot(2 * tick - 1)
-            if tick <= 4:
-                hello(2 * tick - 1)
+            if tick <= NZ // 2:
+                hello()
             hidden_slot(tick, True)
             if tick + AHEAD < NZ:
                 hidden_slot(tick + AHEAD, False)
             weight_slot(2 * tick)
-            if tick <= 4:
-                hello(2 * tick)
+            if tick <= NZ // 2:
+                heard()
             share_tick(tick)
         if tick == 2:
             for copy in local:
@@ -470,23 +525,22 @@
             weight_settle(0)
             settled = 0
             project_first()
-        if tick == 4:
-            send_new(0, near)
-        if tick == 5:
-            send_new(0, rest)
-        if tick == 9:
+        if 3 <= tick <= NZ // 2:
+            away = range(1, 4) if tick == 3 else (tick,)
+            send_new(0, [dz for dz in Z_FAR_FIRST if abs(dz) in away])
+        if tick == 11:
             query_first()
-        if tick == 12:
+        if tick == 14:
             query_first_half()
-        if tick == 13:
-            query_first_rest()
         if tick in PRODUCT_TICKS:
-            upto = tick if tick == NZ - 1 else tick - 1
+            upto = tick - 1
             while settled < NZ // 2 and min(2 * (settled + 1), NZ - 1) <= upto:
                 settled += 1
                 weight_settle(settled)
             products(done, upto)
             done = upto
+    last_products()
+    query_first_rest()
     for slot in (0, 1):
         rows = pl.ds(slot * BLOCK, BLOCK)
         keep = lax.broadcasted_iota(jnp.int32, (BLOCK, BLOCK), 0) < rows_ref[slot]
@@ -545,7 +599,7 @@
     dma = pltpu.SemaphoreType.DMA
     return pl.pallas_call(
         layer_kernel,
-        out_shape=caches + [jax.ShapeDtypeStruct((STEPS, 32, 16), bf16)],
+        out_shape=caches + [jax.ShapeDtypeStruct((STEPS, 16, 32), bf16)],
         in_specs=[smem, smem] + [hbm] * 6,
         out_specs=[any_, any_, pl.BlockSpec(memory_space=pltpu.VMEM)],
         scratch_shapes=[
@@ -597,7 +651,9 @@
     out_specs = (P("cache", "head"), P("cache", "head"), P(None, None, ("cache", "head")))
 
     def on_device(*arrays):
-        return tuple(layer(*arrays))
+        key, value, out = layer(*arrays)
+        low, high = jnp.finfo(key.dtype).min, jnp.finfo(key.dtype).max
+        return lax.clamp(low, key, high), lax.clamp(low, value, high), jnp.swapaxes(out, 1, 2)
 
     return jax.shard_map(
         on_device, mesh=mesh, in_specs=in_specs, out_specs=out_specs, check_vma=False

time: 115 us -> 113 us (0.983)
  local copies, waits for them, and re-layouts: 3.81 us -> 0.6 us
  other arithmetic: 0 us -> 1.87 us
    clamp x0 -> x1, other arithmetic: none -> 1.87 us  [on_device(): lax.clamp(low, value, high)]
    unnamed x4 -> x3, local copies, waits for them, and re-layouts: 2.42 us -> 0.6 us
    pallas_call x1 -> x0, local copies, waits for them, and re-layouts: 1.39 us -> none  [layer(): pl.pallas_call(layer_kernel, out_shape=caches + [jax.ShapeDtypeStruct((ST...]
where the time goes in v3:
time: 113 us; the launch traced here: 112 us
  Pallas kernels  109 us (96%)
  other arithmetic  1.87 us (2%)
    pallas_call x1, Pallas kernels, layer(): pl.pallas_call(layer_kernel, out_shape=caches + [jax.ShapeDtypeStruct((ST...  109 us

profile of v3, /device:TPU:1, one launch (start us, length us, event | category | flops | bytes accessed | tf_op | source)
XLA Modules:
  0.0 112.4 jit_solution(10889646726515771037)
XLA Ops:
  0.6 109.3 %layer.1 = (bf16[512,256]{1,0:T(8,128)(2,1)}, bf16[512,256]{1,0:T(8,128)(2,1)}, bf16[2,16,32]{2,1,0:T(8,128)(2,1)}) custom-call(s32[2]{0:T(128)} %owner_ref.1, s32[2]{0:T(128)} %rows_ref.1, bf16[512,512]{1,0:T(8,128)(2,1)} %hidden_ref.1, bf16[2,2,16,256]{3,2,1,0:T(8,128)(2,1)} %bitcast.2, bf16[256,256]{1,0:T(8,128)(2,1)} %wq_ref.1, bf16[256,256]{1,0:T(8,128)(2,1)} %wk_ref.1, ...), custom_call_target="tpu_custom_call" | custom-call | tf_op jit(solution)/shard_map/layer/pallas_call | solution.py:600
  109.9 0.0 copy-start
  109.9 1.9 %broadcast_clamp_fusion = (bf16[512,256]{1,0:T(8,128)(2,1)}, bf16[512,256]{1,0:T(8,128)(2,1)}) fusion(bf16[512,256]{1,0:T(8,128)(2,1)} %get-tuple-element.7, bf16[512,256]{1,0:T(8,128)(2,1)} %get-tuple-element.6), kind=kLoop, calls=%fused_computation | loop fusion | flops 262144 | bytes 1048576 | tf_op jit(solution)/shard_map/clamp | solution.py:656
  111.8 0.0 copy-done
  111.8 0.6 copy.12
Async XLA Ops:
  109.9 1.9 %copy-start = (bf16[2,16,32]{2,1,0:T(8,128)(2,1)S(1)}, bf16[2,16,32]{2,1,0:T(8,128)(2,1)}, u32[]{:S(2)}) copy-start(bf16[2,16,32]{2,1,0:T(8,128)(2,1)} %get-tuple-element.8) | copy-start | bytes 6148

commit v4 on v3

--- a/solution.py
+++ b/solution.py
@@ -199,7 +199,7 @@
             part = None
             for core in cores:
                 term = jnp.dot(
-                    hbuf[h, :, pl.ds(core * BLOCK, BLOCK)], wbuf[2 * h + core, chunk],
+                    hbuf[h, :, pl.ds(pl.multiple_of(core * BLOCK, BLOCK), BLOCK)], wbuf[2 * h + core, chunk],
                     preferred_element_type=jnp.float32,
                 )
                 part = term if part is None else part + term
@@ -212,18 +212,11 @@
         def _():
             add(corner, (0, 1))
 
-        for core in (0, 1):
-            @pl.when(k == core)
-            def _():
-                add(across, (core,))
-
+        add(across, (k,))
         for part in (0, 1):
             for chunk in (0, 1):
                 have_part(NZ // 2, chunk, part, 1 - k)
-        for core in (0, 1):
-            @pl.when(k != core)
-            def _():
-                add(across, (core,))
+        add(across, (1 - k,))
 
     def products(after, upto):
         def one(h, carry):

time: 113 us -> 112 us (level)
  no operation moved by 1% of the time
where the time goes in v4:
time: 112 us
  Pallas kernels  109 us (97%)
  other arithmetic  1.87 us (2%)
    pallas_call x1, Pallas kernels, layer(): pl.pallas_call(layer_kernel, out_shape=caches + [jax.ShapeDtypeStruct((ST...  109 us

profile of v4, /device:TPU:1, one launch (start us, length us, event | category | flops | bytes accessed | tf_op | source)
XLA Modules:
  0.0 112.2 jit_solution(5299124615992551445)
XLA Ops:
  0.6 109.0 %layer.1 = (bf16[512,256]{1,0:T(8,128)(2,1)}, bf16[512,256]{1,0:T(8,128)(2,1)}, bf16[2,16,32]{2,1,0:T(8,128)(2,1)}) custom-call(s32[2]{0:T(128)} %owner_ref.1, s32[2]{0:T(128)} %rows_ref.1, bf16[512,512]{1,0:T(8,128)(2,1)} %hidden_ref.1, bf16[2,2,16,256]{3,2,1,0:T(8,128)(2,1)} %bitcast.2, bf16[256,256]{1,0:T(8,128)(2,1)} %wq_ref.1, bf16[256,256]{1,0:T(8,128)(2,1)} %wk_ref.1, ...), custom_call_target="tpu_custom_call" | custom-call | tf_op jit(solution)/shard_map/layer/pallas_call | solution.py:593
  109.7 0.0 copy-start
  109.7 1.9 %broadcast_clamp_fusion = (bf16[512,256]{1,0:T(8,128)(2,1)}, bf16[512,256]{1,0:T(8,128)(2,1)}) fusion(bf16[512,256]{1,0:T(8,128)(2,1)} %get-tuple-element.7, bf16[512,256]{1,0:T(8,128)(2,1)} %get-tuple-element.6), kind=kLoop, calls=%fused_computation | loop fusion | flops 262144 | bytes 1048576 | tf_op jit(solution)/shard_map/clamp | solution.py:649
  111.6 0.0 copy-done
  111.6 0.6 copy.12
Async XLA Ops:
  109.7 1.9 %copy-start = (bf16[2,16,32]{2,1,0:T(8,128)(2,1)S(1)}, bf16[2,16,32]{2,1,0:T(8,128)(2,1)}, u32[]{:S(2)}) copy-start(bf16[2,16,32]{2,1,0:T(8,128)(2,1)} %get-tuple-element.8) | copy-start | bytes 6148

commit v5 on v4

--- a/solution.py
+++ b/solution.py
@@ -393,6 +393,8 @@
     def exchange_states(t):
         tag = []
         for i in range(3):
+            if i == 2 and t == 1:
+                new_pair(1)
             mixed, lse = slot_state(i) if i < 2 else new_state(t)
             states[t, k, z, 2 * i : 2 * i + 2, :] = mixed
             tag += [lse[0:1], lse[1:2]]
@@ -553,7 +555,6 @@
     send_new(1)
     remote(opair.at[k, 1 - k], opair.at[k, 1 - k], K_OPAIR, sib)
     query_half(1)
-    new_pair(1)
     departed(qall.at[pl.ds(0, 15)], K_Q)
     departed(qall.at[pl.ds(0, 16)], K_QPAIR)
     query_rest(1)

time: 112 us -> 112 us (level)
  no operation moved by 1% of the time
where the time goes in v5:
time: 112 us
  Pallas kernels  108 us (96%)
  other arithmetic  1.87 us (2%)
    pallas_call x1, Pallas kernels, layer(): pl.pallas_call(layer_kernel, out_shape=caches + [jax.ShapeDtypeStruct((ST...  108 us

profile of v5, /device:TPU:1, one launch (start us, length us, event | category | flops | bytes accessed | tf_op | source)
XLA Modules:
  0.0 111.6 jit_solution(17135165092594712407)
XLA Ops:
  0.6 108.4 %layer.1 = (bf16[512,256]{1,0:T(8,128)(2,1)}, bf16[512,256]{1,0:T(8,128)(2,1)}, bf16[2,16,32]{2,1,0:T(8,128)(2,1)}) custom-call(s32[2]{0:T(128)} %owner_ref.1, s32[2]{0:T(128)} %rows_ref.1, bf16[512,512]{1,0:T(8,128)(2,1)} %hidden_ref.1, bf16[2,2,16,256]{3,2,1,0:T(8,128)(2,1)} %bitcast.2, bf16[256,256]{1,0:T(8,128)(2,1)} %wq_ref.1, bf16[256,256]{1,0:T(8,128)(2,1)} %wk_ref.1, ...), custom_call_target="tpu_custom_call" | custom-call | tf_op jit(solution)/shard_map/layer/pallas_call | solution.py:594
  109.1 0.0 copy-start
  109.1 1.9 %broadcast_clamp_fusion = (bf16[512,256]{1,0:T(8,128)(2,1)}, bf16[512,256]{1,0:T(8,128)(2,1)}) fusion(bf16[512,256]{1,0:T(8,128)(2,1)} %get-tuple-element.7, bf16[512,256]{1,0:T(8,128)(2,1)} %get-tuple-element.6), kind=kLoop, calls=%fused_computation | loop fusion | flops 262144 | bytes 1048576 | tf_op jit(solution)/shard_map/clamp | solution.py:650
  111.0 0.0 copy-done
  111.0 0.6 copy.12
Async XLA Ops:
  109.1 1.9 %copy-start = (bf16[2,16,32]{2,1,0:T(8,128)(2,1)S(1)}, bf16[2,16,32]{2,1,0:T(8,128)(2,1)}, u32[]{:S(2)}) copy-start(bf16[2,16,32]{2,1,0:T(8,128)(2,1)} %get-tuple-element.8) | copy-start | bytes 6148
